TPU v7x, 512 devices: a whole 4x4x16 slice. The times are simulated.
512 devices in a mesh: stream: 4 (over y), frame: 32 (over z, core), head: 4 (over x).
Axes of the slice: x: 4, y: 4, z: 16, core: 2. Of those that a mesh axis runs over, the one named last changes fastest.
Arguments:
- queries: bfloat16 [32768, 3072], P(('stream', 'frame'), 'head'), parts along dimension 0, may hold values from -8 to 8
- keys: bfloat16 [32768, 512], P(('stream', 'frame'), 'head'), parts along dimension 0, may hold values from -8 to 8
- values: bfloat16 [32768, 512], P(('stream', 'frame'), 'head'), parts along dimension 0, may hold values from -6 to 6
- block_mask: int32 [256, 64], P('stream'), parts along dimension 0, may hold values from 0 to 1, as said below
- section_ids: int32 [256], P('stream'), parts along dimension 0, may hold values from 0 to 3
- section_gate: float32 [4, 3072], P(None, 'head'), may hold values from 0.25 to 12
- norm_gain: float32 [3072], P('head'), may hold values from 0.1 to 1.9
Outputs:
- branch_out: bfloat16 [32768, 3072], P(('stream', 'frame'), 'head'), parts along dimension 0
There are 4 independent parts, one for each index of `stream`. A program takes and returns all parts, laid end to end along the dimension named above; an argument that names none is the same for every part. Nothing has to cross between parts.
Inputs may be any that keep to these rules, and one draw needn't show every extreme that they name: `block_mask`: row c is 1 on a run of spans that ends at span c, and 0 elsewhere.
All inputs are finite; a program needn't handle non-finite values.
Results may differ from a plain program's by a relative error of at most 0.017.
Values may be sent and summed in bfloat16 or wider, within the bound.
No kernel may reach another device: no remote copies, remote signals or barrier semaphores. Data moves between devices by JAX's collectives and lax.ppermute only.
A program may use at most 64 MiB of HBM per device.

v0:
```python
import math

import jax
import jax.numpy as jnp
from jax import lax
from jax.sharding import PartitionSpec as P

HEADS = 24
HEAD_DIM = 128


def block_place(block_number, frames):
    owners = block_number // 2
    return jnp.where(block_number % 2 == 0, owners, 2 * frames - 1 - owners)


def absorb(carried_state, query_slot, key_tile, value_tile, live_keys, softmax_scale):
    prior_max, prior_total, prior_sum = carried_state
    scores = (
        jnp.einsum("cgrd,kgd->cgrk", query_slot, key_tile, preferred_element_type=jnp.float32)
        * softmax_scale
    )
    live_wide = live_keys[None, None, None, :]
    scores = jnp.where(live_wide, scores, -1e30)
    new_max = jnp.maximum(prior_max, jnp.max(scores, axis=-1))
    shrink = jnp.exp(prior_max - new_max)
    weights = jnp.where(live_wide, jnp.exp(scores - new_max[..., None]), 0.0)
    new_total = prior_total * shrink + jnp.sum(weights, axis=-1)
    new_sum = prior_sum * shrink[..., None] + jnp.einsum(
        "cgrk,kgd->cgrd",
        weights.astype(jnp.bfloat16),
        value_tile,
        preferred_element_type=jnp.float32,
    )
    return (new_max, new_total, new_sum)


def body(queries, keys, values, block_mask, section_ids, section_gate, norm_gain):
    frames = lax.axis_size("frame")
    frame_index = lax.axis_index("frame")
    local_rows, local_width = queries.shape
    block_rows = local_rows // 2
    kv_local = keys.shape[1] // HEAD_DIM
    head_local = local_width // HEAD_DIM
    group_size = head_local // kv_local
    softmax_scale = HEAD_DIM ** (-0.5)
    own_places = [frame_index, 2 * frames - 1 - frame_index]

    def split_slots(rows_array):
        return [
            rows_array[slot_number * block_rows : (slot_number + 1) * block_rows].reshape(
                block_rows, kv_local, group_size, HEAD_DIM
            )
            for slot_number in range(2)
        ]

    query_slots = split_slots(queries)
    initial = tuple(
        (
            (
                jnp.full((block_rows, kv_local, group_size), -1e30, jnp.float32),
                jnp.zeros((block_rows, kv_local, group_size), jnp.float32),
                jnp.zeros((block_rows, kv_local, group_size, HEAD_DIM), jnp.float32),
            )
            for slot_place in own_places
        )
    )
    run_starts = [slot_place - jnp.sum(block_mask[slot_place]) + 1 for slot_place in own_places]
    key_part = lax.all_gather(keys, "frame", axis=0, tiled=True)
    value_part = lax.all_gather(values, "frame", axis=0, tiled=True)
    piece_rows = key_part.shape[0]
    group_rows = math.gcd(piece_rows, max(1024, 8 * block_rows))
    group_count = piece_rows // group_rows

    def per_group(group_index, carried_states):
        row_start = group_index * group_rows
        key_tile = lax.dynamic_slice_in_dim(key_part, row_start, group_rows, 0).reshape(
            group_rows, kv_local, HEAD_DIM
        )
        value_tile = lax.dynamic_slice_in_dim(value_part, row_start, group_rows, 0).reshape(
            group_rows, kv_local, HEAD_DIM
        )
        row_numbers = row_start + jnp.arange(group_rows, dtype=jnp.int32)
        key_places = block_place(row_numbers // block_rows, frames)
        updated = []
        for query_slot, slot_place, run_start, carried_state in zip(
            query_slots, own_places, run_starts, carried_states
        ):
            live_keys = jnp.logical_and(key_places <= slot_place, key_places >= run_start)
            updated.append(
                lax.cond(
                    jnp.any(live_keys),
                    lambda state_now, query_now=query_slot, live_now=live_keys: absorb(
                        state_now, query_now, key_tile, value_tile, live_now, softmax_scale
                    ),
                    lambda state_now: state_now,
                    carried_state,
                )
            )
        return tuple(updated)

    combined = list(lax.fori_loop(0, group_count, per_group, initial))
    gated_rows = []
    for slot_number in range(2):
        final_max, final_total, final_sum = combined[slot_number]
        normalized = (final_sum / final_total[..., None]).reshape(block_rows, local_width)
        section_now = section_ids[own_places[slot_number]]
        one_hot = (jnp.arange(section_gate.shape[0], dtype=jnp.int32) == section_now).astype(
            jnp.float32
        )
        gate_row = jnp.sum(one_hot[:, None] * section_gate, axis=0)
        gated_rows.append(normalized * gate_row[None, :])
    gated = jnp.concatenate(gated_rows, axis=0)
    squares = lax.psum(jnp.sum(gated * gated, axis=1), "head")
    scale_rows = lax.rsqrt(squares / (HEADS * HEAD_DIM) + 1e-06)
    return (gated * scale_rows[:, None] * norm_gain[None, :]).astype(jnp.bfloat16)


def solution(mesh):
    in_specs = (
        P(("stream", "frame"), "head"),
        P(("stream", "frame"), "head"),
        P(("stream", "frame"), "head"),
        P("stream", None),
        P("stream"),
        P(None, "head"),
        P("head"),
    )
    out_specs = P(("stream", "frame"), "head")
    return jax.shard_map(body, mesh=mesh, in_specs=in_specs, out_specs=out_specs, check_vma=False)
```

profile of v0, /device:TPU:457, one launch (start us, length us, event | category | flops | bytes accessed | tf_op | source)
XLA Modules:
  0.0 245.4 jit_solution(18439526704818654303)
XLA Ops:
  15.9 62.6 %all-gather.3.cloned.1.call-done = bf16[8192,128]{1,0:T(8,128)(2,1)} async-done(((bf16[256,128]{1,0:T(8,128)(2,1)}), bf16[8192,128]{1,0:T(8,128)(2,1)}) %all-gather.3.cloned.1.call-update) | async-done | bytes 2097168 | tf_op jit(solution)/shard_map/all_gather | solution.py:69
  78.5 70.8 %all-gather.5.cloned.1.call-done = bf16[8192,128]{1,0:T(8,128)(2,1)} async-done(((bf16[256,128]{1,0:T(8,128)(2,1)}), bf16[8192,128]{1,0:T(8,128)(2,1)}) %all-gather.5.cloned.1.call-update) | async-done | bytes 2097168 | tf_op jit(solution)/shard_map/all_gather | solution.py:70
  149.4 78.8 %while.26 = (s32[]{:T(128)}, f32[128,1,6]{0,2,1:T(8,128)S(1)}, f32[128,1,6]{0,2,1:T(8,128)S(1)}, f32[128,1,6,128]{3,0,2,1:T(8,128)S(1)}, f32[128,1,6]{0,2,1:T(8,...) while((s32[]{:T(128)}, f32[128,1,6]{0,2,1:T(8,128)S(1)}, ...), condition=%wide.region_13.14_spmd, body=%wide.region_2.13_spmd.sunk | while | flops 826198528 | bytes 23044576 | solution.py:102
  151.9 3.4 %conditional.5 = ((f32[128,1,6]{0,2,1:T(8,128)S(1)}, f32[128,1,6]{0,2,1:T(8,128)S(1)}, f32[128,1,6,128]{3,0,2,1:T(8,128)S(1)})) conditional(s32[]{:T(128)} %convert_element_type.70, (f32[128,1,6]{0,2,1:T(8,128)S(1)}, f32[128,1,6]{0,2,1:T(8,128)S(1)}, f32[128,1,6,128]{3,0,2,1:T(8,128)S(1)}) %tuple.78, (pred[1024]{0:T(1024)(128)(4,1)S(1)}, ...), branch_computations={%region_9.9_spmd, %region_10.12_spmd} | conditional | flops 413075712 | bytes 10996768 | solution.py:91
  155.9 3.4 %conditional.4 = ((f32[128,1,6]{0,2,1:T(8,128)S(1)}, f32[128,1,6]{0,2,1:T(8,128)S(1)}, f32[128,1,6,128]{3,0,2,1:T(8,128)S(1)})) conditional(s32[]{:T(128)} %convert_element_type.69, (f32[128,1,6]{0,2,1:T(8,128)S(1)}, f32[128,1,6]{0,2,1:T(8,128)S(1)}, f32[128,1,6,128]{3,0,2,1:T(8,128)S(1)}) %tuple.76, (pred[1024]{0:T(1024)(128)(4,1)S(1)}, ...), branch_computations={%region_4.4_spmd, %region_5.7_spmd} | conditional | flops 413075712 | bytes 10996768 | solution.py:91
  161.8 3.4 %conditional.5 = ((f32[128,1,6]{0,2,1:T(8,128)S(1)}, f32[128,1,6]{0,2,1:T(8,128)S(1)}, f32[128,1,6,128]{3,0,2,1:T(8,128)S(1)})) conditional(s32[]{:T(128)} %convert_element_type.70, (f32[128,1,6]{0,2,1:T(8,128)S(1)}, f32[128,1,6]{0,2,1:T(8,128)S(1)}, f32[128,1,6,128]{3,0,2,1:T(8,128)S(1)}) %tuple.78, (pred[1024]{0:T(1024)(128)(4,1)S(1)}, ...), branch_computations={%region_9.9_spmd, %region_10.12_spmd} | conditional | flops 413075712 | bytes 10996768 | solution.py:91
  165.7 3.4 %conditional.4 = ((f32[128,1,6]{0,2,1:T(8,128)S(1)}, f32[128,1,6]{0,2,1:T(8,128)S(1)}, f32[128,1,6,128]{3,0,2,1:T(8,128)S(1)})) conditional(s32[]{:T(128)} %convert_element_type.69, (f32[128,1,6]{0,2,1:T(8,128)S(1)}, f32[128,1,6]{0,2,1:T(8,128)S(1)}, f32[128,1,6,128]{3,0,2,1:T(8,128)S(1)}) %tuple.76, (pred[1024]{0:T(1024)(128)(4,1)S(1)}, ...), branch_computations={%region_4.4_spmd, %region_5.7_spmd} | conditional | flops 413075712 | bytes 10996768 | solution.py:91
  171.6 3.4 %conditional.5 = ((f32[128,1,6]{0,2,1:T(8,128)S(1)}, f32[128,1,6]{0,2,1:T(8,128)S(1)}, f32[128,1,6,128]{3,0,2,1:T(8,128)S(1)})) conditional(s32[]{:T(128)} %convert_element_type.70, (f32[128,1,6]{0,2,1:T(8,128)S(1)}, f32[128,1,6]{0,2,1:T(8,128)S(1)}, f32[128,1,6,128]{3,0,2,1:T(8,128)S(1)}) %tuple.78, (pred[1024]{0:T(1024)(128)(4,1)S(1)}, ...), branch_computations={%region_9.9_spmd, %region_10.12_spmd} | conditional | flops 413075712 | bytes 10996768 | solution.py:91
  173.5 1.5 fusion.35
  175.6 3.4 %conditional.4 = ((f32[128,1,6]{0,2,1:T(8,128)S(1)}, f32[128,1,6]{0,2,1:T(8,128)S(1)}, f32[128,1,6,128]{3,0,2,1:T(8,128)S(1)})) conditional(s32[]{:T(128)} %convert_element_type.69, (f32[128,1,6]{0,2,1:T(8,128)S(1)}, f32[128,1,6]{0,2,1:T(8,128)S(1)}, f32[128,1,6,128]{3,0,2,1:T(8,128)S(1)}) %tuple.76, (pred[1024]{0:T(1024)(128)(4,1)S(1)}, ...), branch_computations={%region_4.4_spmd, %region_5.7_spmd} | conditional | flops 413075712 | bytes 10996768 | solution.py:91
  181.5 3.4 %conditional.5 = ((f32[128,1,6]{0,2,1:T(8,128)S(1)}, f32[128,1,6]{0,2,1:T(8,128)S(1)}, f32[128,1,6,128]{3,0,2,1:T(8,128)S(1)})) conditional(s32[]{:T(128)} %convert_element_type.70, (f32[128,1,6]{0,2,1:T(8,128)S(1)}, f32[128,1,6]{0,2,1:T(8,128)S(1)}, f32[128,1,6,128]{3,0,2,1:T(8,128)S(1)}) %tuple.78, (pred[1024]{0:T(1024)(128)(4,1)S(1)}, ...), branch_computations={%region_9.9_spmd, %region_10.12_spmd} | conditional | flops 413075712 | bytes 10996768 | solution.py:91
  183.3 1.5 fusion.35
  185.4 3.4 %conditional.4 = ((f32[128,1,6]{0,2,1:T(8,128)S(1)}, f32[128,1,6]{0,2,1:T(8,128)S(1)}, f32[128,1,6,128]{3,0,2,1:T(8,128)S(1)})) conditional(s32[]{:T(128)} %convert_element_type.69, (f32[128,1,6]{0,2,1:T(8,128)S(1)}, f32[128,1,6]{0,2,1:T(8,128)S(1)}, f32[128,1,6,128]{3,0,2,1:T(8,128)S(1)}) %tuple.76, (pred[1024]{0:T(1024)(128)(4,1)S(1)}, ...), branch_computations={%region_4.4_spmd, %region_5.7_spmd} | conditional | flops 413075712 | bytes 10996768 | solution.py:91
  191.3 3.4 %conditional.5 = ((f32[128,1,6]{0,2,1:T(8,128)S(1)}, f32[128,1,6]{0,2,1:T(8,128)S(1)}, f32[128,1,6,128]{3,0,2,1:T(8,128)S(1)})) conditional(s32[]{:T(128)} %convert_element_type.70, (f32[128,1,6]{0,2,1:T(8,128)S(1)}, f32[128,1,6]{0,2,1:T(8,128)S(1)}, f32[128,1,6,128]{3,0,2,1:T(8,128)S(1)}) %tuple.78, (pred[1024]{0:T(1024)(128)(4,1)S(1)}, ...), branch_computations={%region_9.9_spmd, %region_10.12_spmd} | conditional | flops 413075712 | bytes 10996768 | solution.py:91
  193.2 1.5 fusion.35
  195.3 3.4 %conditional.4 = ((f32[128,1,6]{0,2,1:T(8,128)S(1)}, f32[128,1,6]{0,2,1:T(8,128)S(1)}, f32[128,1,6,128]{3,0,2,1:T(8,128)S(1)})) conditional(s32[]{:T(128)} %convert_element_type.69, (f32[128,1,6]{0,2,1:T(8,128)S(1)}, f32[128,1,6]{0,2,1:T(8,128)S(1)}, f32[128,1,6,128]{3,0,2,1:T(8,128)S(1)}) %tuple.76, (pred[1024]{0:T(1024)(128)(4,1)S(1)}, ...), branch_computations={%region_4.4_spmd, %region_5.7_spmd} | conditional | flops 413075712 | bytes 10996768 | solution.py:91
  201.2 3.4 %conditional.5 = ((f32[128,1,6]{0,2,1:T(8,128)S(1)}, f32[128,1,6]{0,2,1:T(8,128)S(1)}, f32[128,1,6,128]{3,0,2,1:T(8,128)S(1)})) conditional(s32[]{:T(128)} %convert_element_type.70, (f32[128,1,6]{0,2,1:T(8,128)S(1)}, f32[128,1,6]{0,2,1:T(8,128)S(1)}, f32[128,1,6,128]{3,0,2,1:T(8,128)S(1)}) %tuple.78, (pred[1024]{0:T(1024)(128)(4,1)S(1)}, ...), branch_computations={%region_9.9_spmd, %region_10.12_spmd} | conditional | flops 413075712 | bytes 10996768 | solution.py:91
  205.1 3.4 %conditional.4 = ((f32[128,1,6]{0,2,1:T(8,128)S(1)}, f32[128,1,6]{0,2,1:T(8,128)S(1)}, f32[128,1,6,128]{3,0,2,1:T(8,128)S(1)})) conditional(s32[]{:T(128)} %convert_element_type.69, (f32[128,1,6]{0,2,1:T(8,128)S(1)}, f32[128,1,6]{0,2,1:T(8,128)S(1)}, f32[128,1,6,128]{3,0,2,1:T(8,128)S(1)}) %tuple.76, (pred[1024]{0:T(1024)(128)(4,1)S(1)}, ...), branch_computations={%region_4.4_spmd, %region_5.7_spmd} | conditional | flops 413075712 | bytes 10996768 | solution.py:91
  211.0 3.4 %conditional.5 = ((f32[128,1,6]{0,2,1:T(8,128)S(1)}, f32[128,1,6]{0,2,1:T(8,128)S(1)}, f32[128,1,6,128]{3,0,2,1:T(8,128)S(1)})) conditional(s32[]{:T(128)} %convert_element_type.70, (f32[128,1,6]{0,2,1:T(8,128)S(1)}, f32[128,1,6]{0,2,1:T(8,128)S(1)}, f32[128,1,6,128]{3,0,2,1:T(8,128)S(1)}) %tuple.78, (pred[1024]{0:T(1024)(128)(4,1)S(1)}, ...), branch_computations={%region_9.9_spmd, %region_10.12_spmd} | conditional | flops 413075712 | bytes 10996768 | solution.py:91
  212.8 1.5 fusion.35
  214.9 3.4 %conditional.4 = ((f32[128,1,6]{0,2,1:T(8,128)S(1)}, f32[128,1,6]{0,2,1:T(8,128)S(1)}, f32[128,1,6,128]{3,0,2,1:T(8,128)S(1)})) conditional(s32[]{:T(128)} %convert_element_type.69, (f32[128,1,6]{0,2,1:T(8,128)S(1)}, f32[128,1,6]{0,2,1:T(8,128)S(1)}, f32[128,1,6,128]{3,0,2,1:T(8,128)S(1)}) %tuple.76, (pred[1024]{0:T(1024)(128)(4,1)S(1)}, ...), branch_computations={%region_4.4_spmd, %region_5.7_spmd} | conditional | flops 413075712 | bytes 10996768 | solution.py:91
  220.8 3.4 %conditional.5 = ((f32[128,1,6]{0,2,1:T(8,128)S(1)}, f32[128,1,6]{0,2,1:T(8,128)S(1)}, f32[128,1,6,128]{3,0,2,1:T(8,128)S(1)})) conditional(s32[]{:T(128)} %convert_element_type.70, (f32[128,1,6]{0,2,1:T(8,128)S(1)}, f32[128,1,6]{0,2,1:T(8,128)S(1)}, f32[128,1,6,128]{3,0,2,1:T(8,128)S(1)}) %tuple.78, (pred[1024]{0:T(1024)(128)(4,1)S(1)}, ...), branch_computations={%region_9.9_spmd, %region_10.12_spmd} | conditional | flops 413075712 | bytes 10996768 | solution.py:91
  224.8 3.4 %conditional.4 = ((f32[128,1,6]{0,2,1:T(8,128)S(1)}, f32[128,1,6]{0,2,1:T(8,128)S(1)}, f32[128,1,6,128]{3,0,2,1:T(8,128)S(1)})) conditional(s32[]{:T(128)} %convert_element_type.69, (f32[128,1,6]{0,2,1:T(8,128)S(1)}, f32[128,1,6]{0,2,1:T(8,128)S(1)}, f32[128,1,6,128]{3,0,2,1:T(8,128)S(1)}) %tuple.76, (pred[1024]{0:T(1024)(128)(4,1)S(1)}, ...), branch_computations={%region_4.4_spmd, %region_5.7_spmd} | conditional | flops 413075712 | bytes 10996768 | solution.py:91
  229.0 8.4 %psum.7 = f32[256]{0:T(256)S(1)} all-reduce(f32[256]{0:T(256)S(1)} %multiply_reduce_fusion), channel_id=1, replica_groups=mesh['stream'=4,'frame'=32,'head'=4] {'head'}, use_global_device_ids=true, to_apply=%region_17.18 | all-reduce | flops 256 | bytes 2048 | tf_op jit(solution)/shard_map/psum | solution.py:114
  (139 shorter events, 71.5 us)
Async XLA Ops:
  6.5 71.9 %all-gather.3.cloned.1.call-start = ((), (), s32[]{:S(2)}) async-start(), calls=%async_computation | async-start | bytes 2162688 | tf_op jit(solution)/shard_map/all_gather | solution.py:69
  7.3 142.1 %all-gather.5.cloned.1.call-start = ((), (), s32[]{:S(2)}) async-start(), calls=%async_computation.1 | async-start | bytes 2162688 | tf_op jit(solution)/shard_map/all_gather | solution.py:70
  228.2 9.3 %copy-start = (f32[768]{0:T(1024)S(1)}, f32[768]{0:T(1024)}, u32[]{:S(2)}) copy-start(f32[768]{0:T(1024)} %param.19) | copy-start | bytes 9220
Sparse Core Ops, SparseCore 0:
  9.5 68.9 all-gather.2
  80.6 68.6 all-gather.4
where the time goes:
time: 246 us; the launch traced here: 245 us
  waiting for transfers between devices  135 us (55%)
  matrix products  34.8 us (14%)
  other arithmetic  28.3 us (12%)
  between operations  14.8 us (6%)
  local copies, waits for them, and re-layouts  13 us (5%)
  loops' own time  11.2 us (5%)
  blocking collectives  8.41 us (3%)
    all_gather x1, waiting for transfers between devices, body(): value_part = lax.all_gather(values, 'frame', axis=0, tiled=True)  70.8 us
    all_gather x1, waiting for transfers between devices, body(): key_part = lax.all_gather(keys, 'frame', axis=0, tiled=True)  62.6 us
    dot_general x16, matrix products, absorb(): jnp.einsum('cgrk,kgd->cgrd', weights.astype(jnp.bfloat16), value_tile, pr...  24.3 us
    reduce_sum x16, other arithmetic, absorb(): new_total = prior_total * shrink + jnp.sum(weights, axis=-1)  18.1 us
    dot_general x16, matrix products, absorb(): jnp.einsum('cgrd,kgd->cgrk', query_slot, key_tile, preferred_element_type...  10.5 us
    another operation x1, loops' own time, body(): combined = list(lax.fori_loop(0, group_count, per_group, initial))  10.3 us
    reshape x8, local copies, waits for them, and re-layouts, per_group(): lax.dynamic_slice_in_dim(value_part, row_start, group_rows, 0)  8.56 us
    psum x1, blocking collectives, body(): squares = lax.psum(jnp.sum(gated * gated, axis=1), 'head')  8.41 us
  transfers between devices with their start and end apart: 2, of which 2 were waited for; matrix products, arithmetic and copies ran while one was open for 3% of the time, Pallas kernels for 0%

commit v1 on v0

v1 whole, which is shorter than its diff:
```python
import functools
import math

import jax
import jax.numpy as jnp
from jax import lax
from jax.experimental import pallas as pl
from jax.experimental.pallas import tpu as pltpu
from jax.sharding import PartitionSpec as P

HEADS = 24
HEAD_DIM = 128
LOCAL_HEADS = 6
BLOCK = 128
BLOCKS = 64
CHIPS = 16
EPS = 1e-06
TO_LOG2 = HEAD_DIM ** (-0.5) * math.log2(math.e)
LOW = -1e30
VMEM_BYTES = 24 * 1024 * 1024


def attend_body(pieces, first, last, *refs):
    refs = list(refs)
    meta, q_ref = refs.pop(0), refs.pop(0)
    pieces_in = [refs.pop(0) for _ in pieces]
    if not first:
        state_in = [refs.pop(0) for _ in range(3)]
    if last:
        ids_ref, gate_ref = refs.pop(0), refs.pop(0)
        gated_ref, square_ref = refs.pop(0), refs.pop(0)
        acc_ref, sum_ref, max_ref = refs.pop(0), refs.pop(0), refs.pop(0)
    else:
        acc_ref, sum_ref, max_ref = refs.pop(0), refs.pop(0), refs.pop(0)
    buf, table, sems = refs

    copies = []
    tile = 0
    frame = meta[2, 0]
    chip = frame // 2
    core = frame % 2
    for number, ((how, distance), ref) in enumerate(zip(pieces, pieces_in)):
        tiles = ref.shape[0] // 256
        copy = pltpu.make_async_copy(ref, buf.at[pl.ds(tile * 256, tiles * 256)], sems.at[number])
        copy.start()
        copies.append(copy)
        sign = {"own": 0, "mine": -1, "theirs": 1}[how.split("_")[0]]
        source = lax.rem(chip + sign * (1 - 2 * core) * distance + CHIPS, CHIPS)
        if how == "mine_half":
            table[tile, 0], table[tile, 1] = source, core
        elif how == "theirs_half":
            table[tile, 0], table[tile, 1] = source, 1 - core
        else:
            for part in range(2):
                table[tile + part, 0], table[tile + part, 1] = source, jnp.int32(part)
        tile += tiles
    if first:
        acc_ref[...] = jnp.zeros_like(acc_ref)
        sum_ref[...] = jnp.zeros_like(sum_ref)
        max_ref[...] = jnp.full_like(max_ref, LOW)
    else:
        outs = (acc_ref, sum_ref, max_ref)
        for number, (src, dst) in enumerate(zip(state_in, outs)):
            copy = pltpu.make_async_copy(src, dst, sems.at[len(pieces) + number])
            copy.start()
            copies.append(copy)
    for copy in copies:
        copy.wait()

    lane = lax.broadcasted_iota(jnp.int32, (1, 256), 1)
    ones = jnp.ones((256, HEAD_DIM), jnp.bfloat16)

    def step(index, carry):
        slot = index % 2
        number = index // 2
        source, part = table[number, 0], table[number, 1]
        place_a = jnp.where(part == 0, 2 * source, BLOCKS - 1 - 2 * source)
        place_b = jnp.where(part == 0, 2 * source + 1, BLOCKS - 2 - 2 * source)
        live_a, live_b = meta[slot, place_a], meta[slot, place_b]

        @pl.when(live_a + live_b > 0)
        def _():
            rows = pl.ds(pl.multiple_of(slot * BLOCK, BLOCK), BLOCK)
            keys_at = pl.ds(pl.multiple_of(number * 256, 256), 256)
            key_tile = buf[keys_at, :HEAD_DIM]
            value_tile = jnp.concatenate([buf[keys_at, HEAD_DIM:], ones], axis=1)
            low_a = jnp.where(live_a > 0, 0.0, LOW).astype(jnp.float32)
            low_b = jnp.where(live_b > 0, 0.0, LOW).astype(jnp.float32)
            bias = jnp.where(lane < BLOCK, low_a, low_b)
            for head in range(LOCAL_HEADS):
                cols = slice(head * HEAD_DIM, (head + 1) * HEAD_DIM)
                scores = lax.dot_general(
                    q_ref[rows, cols], key_tile, (((1,), (1,)), ((), ())),
                    preferred_element_type=jnp.float32,
                )
                scores = scores * TO_LOG2 + bias
                prior = max_ref[rows, cols]
                now = jnp.maximum(prior, jnp.max(scores, axis=1, keepdims=True))
                weights = jnp.exp2(scores - jnp.concatenate([now, now], axis=1))
                shrink = jnp.exp2(prior - now)
                added = jnp.dot(
                    weights.astype(jnp.bfloat16), value_tile, preferred_element_type=jnp.float32
                )
                acc_ref[rows, cols] = acc_ref[rows, cols] * shrink + added[:, :HEAD_DIM]
                sum_ref[rows, cols] = sum_ref[rows, cols] * shrink + added[:, HEAD_DIM:]
                max_ref[rows, cols] = now

        return carry

    lax.fori_loop(0, 2 * tile, step, 0)

    if last:
        places = (frame, BLOCKS - 1 - frame)
        eye = lax.broadcasted_iota(jnp.int32, (BLOCK, BLOCK), 0) == lax.broadcasted_iota(
            jnp.int32, (BLOCK, BLOCK), 1
        )
        for slot in range(2):
            rows = slice(slot * BLOCK, (slot + 1) * BLOCK)
            gate_row = gate_ref[pl.ds(ids_ref[places[slot]], 1), :]
            total = jnp.zeros((BLOCK, HEAD_DIM), jnp.float32)
            for head in range(LOCAL_HEADS):
                cols = slice(head * HEAD_DIM, (head + 1) * HEAD_DIM)
                gated = acc_ref[rows, cols] / sum_ref[rows, cols] * gate_row[:, cols]
                gated_ref[rows, cols] = gated
                total = total + gated * gated
            row_total = jnp.sum(total, axis=1, keepdims=True)
            square_ref[slot : slot + 1, :] = jnp.sum(
                jnp.where(eye, row_total, 0.0), axis=0, keepdims=True
            )


def attend(pieces, arrays, meta, queries, state, finish=None):
    first, last = state is None, finish is not None
    tiles = sum(array.shape[0] // 256 for array in arrays)
    rows, cols = queries.shape
    wide = jax.ShapeDtypeStruct((rows, cols), jnp.float32)
    vmem, smem, anywhere = (
        pl.BlockSpec(memory_space=pltpu.VMEM),
        pl.BlockSpec(memory_space=pltpu.SMEM),
        pl.BlockSpec(memory_space=pl.ANY),
    )
    operands = [meta, queries, *arrays]
    in_specs = [smem, vmem] + [anywhere] * len(arrays)
    scratch = [
        pltpu.VMEM((tiles * 256, 256), jnp.bfloat16),
        pltpu.SMEM((max(tiles, 2), 2), jnp.int32),
        pltpu.SemaphoreType.DMA((len(arrays) + 3,)),
    ]
    if not first:
        operands += list(state)
        in_specs += [anywhere] * 3
    if last:
        operands += list(finish)
        in_specs += [smem, vmem]
        out_shape = [wide, jax.ShapeDtypeStruct((2, BLOCK), jnp.float32)]
        scratch = [pltpu.VMEM((rows, cols), jnp.float32)] * 3 + scratch
    else:
        out_shape = [wide] * 3
    pairs = tiles * 2 * LOCAL_HEADS
    return pl.pallas_call(
        functools.partial(attend_body, pieces, first, last),
        out_shape=out_shape,
        in_specs=in_specs,
        out_specs=[vmem] * len(out_shape),
        scratch_shapes=scratch,
        compiler_params=pltpu.CompilerParams(vmem_limit_bytes=VMEM_BYTES),
        cost_estimate=pl.CostEstimate(
            flops=pairs * 4 * BLOCK * 256 * HEAD_DIM,
            bytes_accessed=8 * rows * cols * 4,
            transcendentals=pairs * BLOCK * 256,
        ),
    )(*operands)


def gather_pair_body(core_ref, own_ref, other_ref, out_ref):
    core = core_ref[2, 0] % 2
    for half in range(2):
        at = 256 * half
        out_ref[pl.ds(pl.multiple_of(at + 128 * core, 128), 128), :] = own_ref[half * 128 : half * 128 + 128, :]
        out_ref[pl.ds(pl.multiple_of(at + 128 * (1 - core), 128), 128), :] = other_ref[half * 128 : half * 128 + 128, :]


def gather_pair(meta, own, other):
    return pl.pallas_call(
        gather_pair_body,
        out_shape=jax.ShapeDtypeStruct((512, 256), jnp.bfloat16),
        in_specs=[pl.BlockSpec(memory_space=pltpu.SMEM)] + [pl.BlockSpec(memory_space=pltpu.VMEM)] * 2,
        out_specs=pl.BlockSpec(memory_space=pltpu.VMEM),
        compiler_params=pltpu.CompilerParams(vmem_limit_bytes=VMEM_BYTES),
    )(meta, own, other)


def scale_body(gated_ref, square_ref, gain_ref, out_ref):
    eye = lax.broadcasted_iota(jnp.int32, (BLOCK, BLOCK), 0) == lax.broadcasted_iota(
        jnp.int32, (BLOCK, BLOCK), 1
    )
    for slot in range(2):
        rows = slice(slot * BLOCK, (slot + 1) * BLOCK)
        scale = lax.rsqrt(square_ref[slot : slot + 1, :] / (HEADS * HEAD_DIM) + EPS)
        column = jnp.sum(jnp.where(eye, scale, 0.0), axis=1, keepdims=True)
        out_ref[rows, :] = (gated_ref[rows, :] * column * gain_ref[...]).astype(jnp.bfloat16)


def scale_rows(gated, squares, gain):
    return pl.pallas_call(
        scale_body,
        out_shape=jax.ShapeDtypeStruct(gated.shape, jnp.bfloat16),
        in_specs=[pl.BlockSpec(memory_space=pltpu.VMEM)] * 3,
        out_specs=pl.BlockSpec(memory_space=pltpu.VMEM),
        compiler_params=pltpu.CompilerParams(vmem_limit_bytes=VMEM_BYTES),
    )(gated, squares, gain)


def along(hops):
    return [(2 * z, 2 * ((z + hops) % CHIPS)) for z in range(CHIPS)] + [
        (2 * z + 1, 2 * ((z - hops) % CHIPS) + 1) for z in range(CHIPS)
    ]


def send(array, hops):
    return lax.ppermute(array, "frame", along(hops))


def swap(array):
    return lax.ppermute(array, "frame", [(d, d ^ 1) for d in range(2 * CHIPS)])


def body(queries, keys, values, block_mask, section_ids, section_gate, norm_gain):
    frame = lax.axis_index("frame")
    own = jnp.concatenate([keys, values], axis=1)
    meta = jnp.concatenate(
        [
            lax.dynamic_slice_in_dim(block_mask, frame, 1, 0),
            lax.dynamic_slice_in_dim(block_mask, BLOCKS - 1 - frame, 1, 0),
            jnp.full((1, BLOCKS), frame, jnp.int32),
        ],
        axis=0,
    )
    core = frame % 2
    chunk = gather_pair(meta, own, swap(own))

    s3 = send(chunk, 3)
    s1 = send(chunk, 1)
    s2 = send(chunk, 2)
    state = attend([("own", 0)], [chunk], meta, queries, None)

    s6 = send(s3, 3)
    s4 = send(s3, 1)
    s5 = send(s3, 2)
    w123 = swap(jnp.concatenate([s1, s2, s3], axis=0))
    state = attend([("mine", 1), ("mine", 2), ("mine", 3)], [s1, s2, s3], meta, queries, state)
    w123 = [w123[512 * i : 512 * i + 512] for i in range(3)]
    state = attend([("theirs", 1), ("theirs", 2), ("theirs", 3)], w123, meta, queries, state)

    s7 = send(s6, 1)
    half = lax.dynamic_slice_in_dim(s6, 256 * core, 256, 0)
    s8 = send(half, 2)
    w456 = swap(jnp.concatenate([s4, s5, s6], axis=0))
    state = attend([("mine", 4), ("mine", 5), ("mine", 6)], [s4, s5, s6], meta, queries, state)
    w456 = [w456[512 * i : 512 * i + 512] for i in range(3)]
    state = attend([("theirs", 4), ("theirs", 5), ("theirs", 6)], w456, meta, queries, state)

    w78 = swap(jnp.concatenate([s7, s8], axis=0))
    state = attend([("mine", 7), ("mine_half", 8)], [s7, s8], meta, queries, state)
    gated, squares = attend(
        [("theirs", 7), ("theirs_half", 8)],
        [w78[:512], w78[512:]],
        meta,
        queries,
        state,
        (section_ids, section_gate),
    )
    squares = lax.psum(squares, "head")
    return scale_rows(gated, squares, norm_gain.reshape(1, -1))


def solution(mesh):
    in_specs = (
        P(("stream", "frame"), "head"),
        P(("stream", "frame"), "head"),
        P(("stream", "frame"), "head"),
        P("stream", None),
        P("stream"),
        P(None, "head"),
        P("head"),
    )
    out_specs = P(("stream", "frame"), "head")
    return jax.shard_map(body, mesh=mesh, in_specs=in_specs, out_specs=out_specs, check_vma=False)
```

time: 246 us -> 101 us (0.41)
  the two profiles are of different devices: /device:TPU:457 before, /device:TPU:24 now
where the time goes in v1:
time: 101 us; the launch traced here: 99.1 us
  starting transfers between devices  48 us (48%)
  Pallas kernels  24.5 us (24%)
  waiting for transfers between devices  12.8 us (13%)
  blocking collectives  10.5 us (10%)
  local copies, waits for them, and re-layouts  2.68 us (3%)
    ppermute x8, starting transfers between devices, send(): return lax.ppermute(array, 'frame', along(hops))  37.3 us
    pallas_call x7, Pallas kernels, attend(): pl.pallas_call(functools.partial(attend_body, pieces, first, last), out_s...  23 us
    ppermute x8, waiting for transfers between devices, send(): return lax.ppermute(array, 'frame', along(hops))  12.3 us
    ppermute x4, starting transfers between devices, swap(): return lax.ppermute(array, 'frame', [(d, d ^ 1) for d in range(2 * CHIPS)])  10.7 us
    psum x1, blocking collectives, body(): squares = lax.psum(squares, 'head')  10.5 us
  transfers between devices with their start and end apart: 12, of which 5 were waited for; matrix products, arithmetic and copies ran while one was open for 1% of the time, Pallas kernels for 14%

profile of v1, /device:TPU:24, one launch (start us, length us, event | category | flops | bytes accessed | tf_op | source)
XLA Modules:
  0.0 99.1 jit_solution(14476034079607894374)
XLA Ops:
  1.7 1.9 %collective-permute-start = (bf16[256,256]{1,0:T(8,128)(2,1)S(1)}, bf16[256,256]{1,0:T(8,128)(2,1)S(1)}, u32[]{:S(2)}, u32[]{:S(2)}) collective-permute-start(bf16[256,256]{1,0:T(8,128)(2,1)S(1)} %constant_dynamic-update-slice_fusion.own_ref), channel_id=1, source_target_pairs={{0,4},{4,0},{8,12},{12,8},{16,20},{20,16},{24,28},{28,24},{32,36},... | collective-permute-start | bytes 393224 | tf_op jit(solution)/shard_map/ppermute | solution.py:225
  5.6 6.5 %collective-permute-start.1 = (bf16[512,256]{1,0:T(8,128)(2,1)S(1)}, bf16[512,256]{1,0:T(8,128)(2,1)S(1)}, u32[]{:S(2)}, u32[]{:S(2)}) collective-permute-start(bf16[512,256]{1,0:T(8,128)(2,1)S(1)} %shard_map.73.refs_2_), channel_id=1, source_target_pairs={{0,24},{8,32},{16,40},{24,48},{32,56},{40,64},{48,72},{56,80},{64,... | collective-permute-start | bytes 786440 | tf_op jit(solution)/shard_map/ppermute | solution.py:221
  12.1 6.4 %collective-permute-start.10 = (bf16[512,256]{1,0:T(8,128)(2,1)S(1)}, bf16[512,256]{1,0:T(8,128)(2,1)S(1)}, u32[]{:S(2)}, u32[]{:S(2)}) collective-permute-start(bf16[512,256]{1,0:T(8,128)(2,1)S(1)} %shard_map.73.refs_2_), channel_id=1, source_target_pairs={{0,16},{8,24},{16,32},{24,40},{32,48},{40,56},{48,64},{56,72},{64,... | collective-permute-start | bytes 786440 | tf_op jit(solution)/shard_map/ppermute | solution.py:221
  18.5 3.8 %collective-permute-start.9 = (bf16[512,256]{1,0:T(8,128)(2,1)S(1)}, bf16[512,256]{1,0:T(8,128)(2,1)S(1)}, u32[]{:S(2)}, u32[]{:S(2)}) collective-permute-start(bf16[512,256]{1,0:T(8,128)(2,1)S(1)} %shard_map.73.refs_2_), channel_id=1, source_target_pairs={{0,8},{8,16},{16,24},{24,32},{32,40},{40,48},{48,56},{56,64},{64,7... | collective-permute-start | bytes 786440 | tf_op jit(solution)/shard_map/ppermute | solution.py:221
  22.3 2.4 %collective-permute-done.1.refs_4_ = bf16[512,256]{1,0:T(8,128)(2,1)S(1)} collective-permute-done((bf16[512,256]{1,0:T(8,128)(2,1)S(1)}, bf16[512,256]{1,0:T(8,128)(2,1)S(1)}, u32[]{:S(2)}, u32[]{:S(2)}) %collective-permute-start.1) | collective-permute-done | bytes 262176 | tf_op jit(solution)/shard_map/ppermute | solution.py:221
  24.8 6.5 %collective-permute-start.2 = (bf16[512,256]{1,0:T(8,128)(2,1)S(1)}, bf16[512,256]{1,0:T(8,128)(2,1)S(1)}, u32[]{:S(2)}, u32[]{:S(2)}) collective-permute-start(bf16[512,256]{1,0:T(8,128)(2,1)S(1)} %collective-permute-done.1.refs_4_), channel_id=1, source_target_pairs={{0,24},{8,32},{16,40},{24,48},{32,56},{40,64},{48,72},{56,80},{64,... | collective-permute-start | bytes 786440 | tf_op jit(solution)/shard_map/ppermute | solution.py:221
  31.3 1.9 %collective-permute-start.6 = (bf16[512,256]{1,0:T(8,128)(2,1)S(1)}, bf16[512,256]{1,0:T(8,128)(2,1)S(1)}, u32[]{:S(2)}, u32[]{:S(2)}) collective-permute-start(bf16[512,256]{1,0:T(8,128)(2,1)S(1)} %collective-permute-done.1.refs_4_), channel_id=1, source_target_pairs={{0,8},{8,16},{16,24},{24,32},{32,40},{40,48},{48,56},{56,64},{64,7... | collective-permute-start | bytes 786440 | tf_op jit(solution)/shard_map/ppermute | solution.py:221
  33.2 8.0 %collective-permute-start.7 = (bf16[512,256]{1,0:T(8,128)(2,1)S(1)}, bf16[512,256]{1,0:T(8,128)(2,1)S(1)}, u32[]{:S(2)}, u32[]{:S(2)}) collective-permute-start(bf16[512,256]{1,0:T(8,128)(2,1)S(1)} %collective-permute-done.1.refs_4_), channel_id=1, source_target_pairs={{0,16},{8,24},{16,32},{24,40},{32,48},{40,56},{48,64},{56,72},{64,... | collective-permute-start | bytes 786440 | tf_op jit(solution)/shard_map/ppermute | solution.py:221
  41.3 1.9 %collective-permute-start.11 = (bf16[1536,256]{1,0:T(8,128)(2,1)S(1)}, bf16[1536,256]{1,0:T(8,128)(2,1)S(1)}, u32[]{:S(2)}, u32[]{:S(2)}) collective-permute-start(bf16[1536,256]{1,0:T(8,128)(2,1)S(1)} %pad_maximum_fusion.1), channel_id=1, source_target_pairs={{0,4},{4,0},{8,12},{12,8},{16,20},{20,16},{24,28},{28,24},{32,36},... | collective-permute-start | bytes 2359304 | tf_op jit(solution)/shard_map/ppermute | solution.py:225
  43.3 3.5 %collective-permute-done.6.refs_2_ = bf16[512,256]{1,0:T(8,128)(2,1)S(1)} collective-permute-done((bf16[512,256]{1,0:T(8,128)(2,1)S(1)}, bf16[512,256]{1,0:T(8,128)(2,1)S(1)}, u32[]{:S(2)}, u32[]{:S(2)}) %collective-permute-start.6) | collective-permute-done | bytes 262176 | tf_op jit(solution)/shard_map/ppermute | solution.py:221
  46.7 6.1 %collective-permute-done.7.refs_3_ = bf16[512,256]{1,0:T(8,128)(2,1)S(1)} collective-permute-done((bf16[512,256]{1,0:T(8,128)(2,1)S(1)}, bf16[512,256]{1,0:T(8,128)(2,1)S(1)}, u32[]{:S(2)}, u32[]{:S(2)}) %collective-permute-start.7) | collective-permute-done | bytes 262176 | tf_op jit(solution)/shard_map/ppermute | solution.py:221
  52.9 1.9 %collective-permute-start.8 = (bf16[1536,256]{1,0:T(8,128)(2,1)S(1)}, bf16[1536,256]{1,0:T(8,128)(2,1)S(1)}, u32[]{:S(2)}, u32[]{:S(2)}) collective-permute-start(bf16[1536,256]{1,0:T(8,128)(2,1)S(1)} %pad_maximum_fusion), channel_id=1, source_target_pairs={{0,4},{4,0},{8,12},{12,8},{16,20},{20,16},{24,28},{28,24},{32,36},... | collective-permute-start | bytes 2359304 | tf_op jit(solution)/shard_map/ppermute | solution.py:225
  54.9 1.9 %collective-permute-start.3 = (bf16[512,256]{1,0:T(8,128)(2,1)S(1)}, bf16[512,256]{1,0:T(8,128)(2,1)S(1)}, u32[]{:S(2)}, u32[]{:S(2)}) collective-permute-start(bf16[512,256]{1,0:T(8,128)(2,1)S(1)} %collective-permute-done.2.refs_4_), channel_id=1, source_target_pairs={{0,8},{8,16},{16,24},{24,32},{32,40},{40,48},{48,56},{56,64},{64,7... | collective-permute-start | bytes 786440 | tf_op jit(solution)/shard_map/ppermute | solution.py:221
  56.8 2.3 %collective-permute-start.4 = (bf16[256,256]{1,0:T(8,128)(2,1)S(1)}, bf16[256,256]{1,0:T(8,128)(2,1)S(1)}, u32[]{:S(2)}, u32[]{:S(2)}) collective-permute-start(bf16[256,256]{1,0:T(8,128)(2,1)S(1)} %constant_dynamic-slice_fusion), channel_id=1, source_target_pairs={{0,16},{8,24},{16,32},{24,40},{32,48},{40,56},{48,64},{56,72},{64,... | collective-permute-start | bytes 393224 | tf_op jit(solution)/shard_map/ppermute | solution.py:221
  59.1 2.0 %shard_map.74 = (f32[256,768]{1,0:T(8,128)S(1)}, f32[256,768]{1,0:T(8,128)S(1)}, f32[256,768]{1,0:T(8,128)S(1)}) custom-call(s32[3,64]{1,0:T(4,128)S(1)} %add_add_fusion.core_ref.refs_0_, bf16[256,768]{1,0:T(8,128)(2,1)S(1)} %copy-done, bf16[512,256]{1,0:T(8,128)(2,1)S(1)} %shard_map.73.refs_2_), custom_call_target="tpu_custom_call" | custom-call | flops 402653184 | bytes 6291456 | tf_op jit(solution)/shard_map/pallas_call | solution.py:160
  61.1 4.6 %shard_map.75 = (f32[256,768]{1,0:T(8,128)S(1)}, f32[256,768]{1,0:T(8,128)S(1)}, f32[256,768]{1,0:T(8,128)S(1)}) custom-call(s32[3,64]{1,0:T(4,128)S(1)} %add_add_fusion.core_ref.refs_0_, bf16[256,768]{1,0:T(8,128)(2,1)S(1)} %copy-done, bf16[512,256]{1,0:T(8,128)(2,1)S(1)} %collective-permute-done.9.refs_2_, ...), custom_call_target="tpu_custom_call" | custom-call | flops 1207959552 | bytes 6291456 | tf_op jit(solution)/shard_map/pallas_call | solution.py:160
  66.0 5.0 %collective-permute-start.5 = (bf16[768,256]{1,0:T(8,128)(2,1)S(1)}, bf16[768,256]{1,0:T(8,128)(2,1)S(1)}, u32[]{:S(2)}, u32[]{:S(2)}) collective-permute-start(bf16[768,256]{1,0:T(8,128)(2,1)S(1)} %pad_maximum_fusion.2), channel_id=1, source_target_pairs={{0,4},{4,0},{8,12},{12,8},{16,20},{20,16},{24,28},{28,24},{32,36},... | collective-permute-start | bytes 1179656 | tf_op jit(solution)/shard_map/ppermute | solution.py:225
  71.1 2.9 %shard_map.76 = (f32[256,768]{1,0:T(8,128)S(1)}, f32[256,768]{1,0:T(8,128)S(1)}, f32[256,768]{1,0:T(8,128)S(1)}) custom-call(s32[3,64]{1,0:T(4,128)S(1)} %add_add_fusion.core_ref.refs_0_, bf16[256,768]{1,0:T(8,128)(2,1)S(1)} %copy-done, bf16[512,256]{1,0:T(8,128)(2,1)S(1)} %get-tuple-element.47.refs_2_, bf16[512,256]{1,0:T(8,128)(2,1)S(1)} %get-tuple-element.46.refs_3_, ...), custom_call_target="tpu_custom_call" | custom-call | flops 1207959552 | bytes 6291456 | tf_op jit(solution)/shard_map/pallas_call | solution.py:160
  74.0 4.6 %shard_map.77 = (f32[256,768]{1,0:T(8,128)S(1)}, f32[256,768]{1,0:T(8,128)S(1)}, f32[256,768]{1,0:T(8,128)S(1)}) custom-call(s32[3,64]{1,0:T(4,128)S(1)} %add_add_fusion.core_ref.refs_0_, bf16[256,768]{1,0:T(8,128)(2,1)S(1)} %copy-done, bf16[512,256]{1,0:T(8,128)(2,1)S(1)} %collective-permute-done.6.refs_2_, ...), custom_call_target="tpu_custom_call" | custom-call | flops 1207959552 | bytes 6291456 | tf_op jit(solution)/shard_map/pallas_call | solution.py:160
  78.7 2.9 %shard_map.78 = (f32[256,768]{1,0:T(8,128)S(1)}, f32[256,768]{1,0:T(8,128)S(1)}, f32[256,768]{1,0:T(8,128)S(1)}) custom-call(s32[3,64]{1,0:T(4,128)S(1)} %add_add_fusion.core_ref.refs_0_, bf16[256,768]{1,0:T(8,128)(2,1)S(1)} %copy-done, bf16[512,256]{1,0:T(8,128)(2,1)S(1)} %get-tuple-element.50.refs_2_, bf16[512,256]{1,0:T(8,128)(2,1)S(1)} %get-tuple-element.49.refs_3_, ...), custom_call_target="tpu_custom_call" | custom-call | flops 1207959552 | bytes 6291456 | tf_op jit(solution)/shard_map/pallas_call | solution.py:160
  81.7 2.9 %shard_map.79 = (f32[256,768]{1,0:T(8,128)S(1)}, f32[256,768]{1,0:T(8,128)S(1)}, f32[256,768]{1,0:T(8,128)S(1)}) custom-call(s32[3,64]{1,0:T(4,128)S(1)} %add_add_fusion.core_ref.refs_0_, bf16[256,768]{1,0:T(8,128)(2,1)S(1)} %copy-done, bf16[512,256]{1,0:T(8,128)(2,1)S(1)} %collective-permute-done.3.refs_2_, ...), custom_call_target="tpu_custom_call" | custom-call | flops 603979776 | bytes 6291456 | tf_op jit(solution)/shard_map/pallas_call | solution.py:160
  84.6 3.1 %shard_map.80 = (f32[256,768]{1,0:T(8,128)S(1)}, f32[2,128]{1,0:T(2,128)S(1)}) custom-call(s32[3,64]{1,0:T(4,128)S(1)} %add_add_fusion.core_ref.refs_0_, bf16[256,768]{1,0:T(8,128)(2,1)S(1)} %copy-done, bf16[512,256]{1,0:T(8,128)(2,1)S(1)} %slice.32.refs_2_, bf16[256,256]{1,0:T(8,128)(2,1)S(1)} %slice.33.refs_3_, f32[256,768]{1,0:T(8,128)S(1)} %get-tuple-element.40.refs_4_, ...), custom_call_target="tpu_custom_call" | custom-call | flops 603979776 | bytes 6291456 | tf_op jit(solution)/shard_map/pallas_call | solution.py:160
  87.7 10.5 %psum.7.square_ref = f32[2,128]{1,0:T(2,128)S(1)} all-reduce(f32[2,128]{1,0:T(2,128)S(1)} %get-tuple-element.44), channel_id=1, replica_groups=mesh['stream'=4,'frame'=32,'head'=4] {'head'}, use_global_device_ids=true, to_apply=%region_0.1 | all-reduce | flops 256 | bytes 2048 | tf_op jit(solution)/shard_map/psum | solution.py:273
  98.1 0.9 shard_map.81
  (32 shorter events, 4.2 us)
Async XLA Ops:
  1.7 3.2 %collective-permute-start = (bf16[256,256]{1,0:T(8,128)(2,1)S(1)}, bf16[256,256]{1,0:T(8,128)(2,1)S(1)}, u32[]{:S(2)}, u32[]{:S(2)}) collective-permute-start(bf16[256,256]{1,0:T(8,128)(2,1)S(1)} %constant_dynamic-update-slice_fusion.own_ref), channel_id=1, source_target_pairs={{0,4},{4,0},{8,12},{12,8},{16,20},{20,16},{24,28},{28,24},{32,36},... | collective-permute-start | bytes 393224 | tf_op jit(solution)/shard_map/ppermute | solution.py:225
  5.6 37.7 %copy-start.3 = (f32[768]{0:T(1024)S(1)}, f32[768]{0:T(1024)}, u32[]{:S(2)}) copy-start(f32[768]{0:T(1024)} %param.13) | copy-start | bytes 9220
  5.6 19.2 %collective-permute-start.1 = (bf16[512,256]{1,0:T(8,128)(2,1)S(1)}, bf16[512,256]{1,0:T(8,128)(2,1)S(1)}, u32[]{:S(2)}, u32[]{:S(2)}) collective-permute-start(bf16[512,256]{1,0:T(8,128)(2,1)S(1)} %shard_map.73.refs_2_), channel_id=1, source_target_pairs={{0,24},{8,32},{16,40},{24,48},{32,56},{40,64},{48,72},{56,80},{64,... | collective-permute-start | bytes 786440 | tf_op jit(solution)/shard_map/ppermute | solution.py:221
  12.1 29.1 %collective-permute-start.10 = (bf16[512,256]{1,0:T(8,128)(2,1)S(1)}, bf16[512,256]{1,0:T(8,128)(2,1)S(1)}, u32[]{:S(2)}, u32[]{:S(2)}) collective-permute-start(bf16[512,256]{1,0:T(8,128)(2,1)S(1)} %shard_map.73.refs_2_), channel_id=1, source_target_pairs={{0,16},{8,24},{16,32},{24,40},{32,48},{40,56},{48,64},{56,72},{64,... | collective-permute-start | bytes 786440 | tf_op jit(solution)/shard_map/ppermute | solution.py:221
  18.5 22.7 %collective-permute-start.9 = (bf16[512,256]{1,0:T(8,128)(2,1)S(1)}, bf16[512,256]{1,0:T(8,128)(2,1)S(1)}, u32[]{:S(2)}, u32[]{:S(2)}) collective-permute-start(bf16[512,256]{1,0:T(8,128)(2,1)S(1)} %shard_map.73.refs_2_), channel_id=1, source_target_pairs={{0,8},{8,16},{16,24},{24,32},{32,40},{40,48},{48,56},{56,64},{64,7... | collective-permute-start | bytes 786440 | tf_op jit(solution)/shard_map/ppermute | solution.py:221
  24.8 18.5 %collective-permute-start.2 = (bf16[512,256]{1,0:T(8,128)(2,1)S(1)}, bf16[512,256]{1,0:T(8,128)(2,1)S(1)}, u32[]{:S(2)}, u32[]{:S(2)}) collective-permute-start(bf16[512,256]{1,0:T(8,128)(2,1)S(1)} %collective-permute-done.1.refs_4_), channel_id=1, source_target_pairs={{0,24},{8,32},{16,40},{24,48},{32,56},{40,64},{48,72},{56,80},{64,... | collective-permute-start | bytes 786440 | tf_op jit(solution)/shard_map/ppermute | solution.py:221
  31.3 15.4 %collective-permute-start.6 = (bf16[512,256]{1,0:T(8,128)(2,1)S(1)}, bf16[512,256]{1,0:T(8,128)(2,1)S(1)}, u32[]{:S(2)}, u32[]{:S(2)}) collective-permute-start(bf16[512,256]{1,0:T(8,128)(2,1)S(1)} %collective-permute-done.1.refs_4_), channel_id=1, source_target_pairs={{0,8},{8,16},{16,24},{24,32},{32,40},{40,48},{48,56},{56,64},{64,7... | collective-permute-start | bytes 786440 | tf_op jit(solution)/shard_map/ppermute | solution.py:221
  33.2 19.6 %collective-permute-start.7 = (bf16[512,256]{1,0:T(8,128)(2,1)S(1)}, bf16[512,256]{1,0:T(8,128)(2,1)S(1)}, u32[]{:S(2)}, u32[]{:S(2)}) collective-permute-start(bf16[512,256]{1,0:T(8,128)(2,1)S(1)} %collective-permute-done.1.refs_4_), channel_id=1, source_target_pairs={{0,16},{8,24},{16,32},{24,40},{32,48},{40,56},{48,64},{56,72},{64,... | collective-permute-start | bytes 786440 | tf_op jit(solution)/shard_map/ppermute | solution.py:221
  41.3 29.7 %collective-permute-start.11 = (bf16[1536,256]{1,0:T(8,128)(2,1)S(1)}, bf16[1536,256]{1,0:T(8,128)(2,1)S(1)}, u32[]{:S(2)}, u32[]{:S(2)}) collective-permute-start(bf16[1536,256]{1,0:T(8,128)(2,1)S(1)} %pad_maximum_fusion.1), channel_id=1, source_target_pairs={{0,4},{4,0},{8,12},{12,8},{16,20},{20,16},{24,28},{28,24},{32,36},... | collective-permute-start | bytes 2359304 | tf_op jit(solution)/shard_map/ppermute | solution.py:225
  43.3 15.8 %copy-start = (bf16[256,768]{1,0:T(8,128)(2,1)S(1)}, bf16[256,768]{1,0:T(8,128)(2,1)}, u32[]{:S(2)}) copy-start(bf16[256,768]{1,0:T(8,128)(2,1)} %refs_1_.13) | copy-start | bytes 1179652
  52.9 25.7 %collective-permute-start.8 = (bf16[1536,256]{1,0:T(8,128)(2,1)S(1)}, bf16[1536,256]{1,0:T(8,128)(2,1)S(1)}, u32[]{:S(2)}, u32[]{:S(2)}) collective-permute-start(bf16[1536,256]{1,0:T(8,128)(2,1)S(1)} %pad_maximum_fusion), channel_id=1, source_target_pairs={{0,4},{4,0},{8,12},{12,8},{16,20},{20,16},{24,28},{28,24},{32,36},... | collective-permute-start | bytes 2359304 | tf_op jit(solution)/shard_map/ppermute | solution.py:225
  54.9 11.1 %collective-permute-start.3 = (bf16[512,256]{1,0:T(8,128)(2,1)S(1)}, bf16[512,256]{1,0:T(8,128)(2,1)S(1)}, u32[]{:S(2)}, u32[]{:S(2)}) collective-permute-start(bf16[512,256]{1,0:T(8,128)(2,1)S(1)} %collective-permute-done.2.refs_4_), channel_id=1, source_target_pairs={{0,8},{8,16},{16,24},{24,32},{32,40},{40,48},{48,56},{56,64},{64,7... | collective-permute-start | bytes 786440 | tf_op jit(solution)/shard_map/ppermute | solution.py:221
  56.8 9.2 %collective-permute-start.4 = (bf16[256,256]{1,0:T(8,128)(2,1)S(1)}, bf16[256,256]{1,0:T(8,128)(2,1)S(1)}, u32[]{:S(2)}, u32[]{:S(2)}) collective-permute-start(bf16[256,256]{1,0:T(8,128)(2,1)S(1)} %constant_dynamic-slice_fusion), channel_id=1, source_target_pairs={{0,16},{8,24},{16,32},{24,40},{32,48},{40,56},{48,64},{56,72},{64,... | collective-permute-start | bytes 393224 | tf_op jit(solution)/shard_map/ppermute | solution.py:221
  66.0 12.6 %collective-permute-start.5 = (bf16[768,256]{1,0:T(8,128)(2,1)S(1)}, bf16[768,256]{1,0:T(8,128)(2,1)S(1)}, u32[]{:S(2)}, u32[]{:S(2)}) collective-permute-start(bf16[768,256]{1,0:T(8,128)(2,1)S(1)} %pad_maximum_fusion.2), channel_id=1, source_target_pairs={{0,4},{4,0},{8,12},{12,8},{16,20},{20,16},{24,28},{28,24},{32,36},... | collective-permute-start | bytes 1179656 | tf_op jit(solution)/shard_map/ppermute | solution.py:225
  81.7 2.9 %copy-start.1 = (f32[4,768]{1,0:T(4,128)S(1)}, f32[4,768]{1,0:T(4,128)}, u32[]{:S(2)}) copy-start(f32[4,768]{1,0:T(4,128)} %refs_8_.1) | copy-start | bytes 36868
  81.7 2.9 %copy-start.2 = (s32[64]{0:T(128)S(1)}, s32[64]{0:T(128)}, u32[]{:S(2)}) copy-start(s32[64]{0:T(128)} %refs_7_.1) | copy-start | bytes 772

commit v2 on v1

v2 whole, which is shorter than its diff:
```python
import functools
import math

import jax
import jax.numpy as jnp
from jax import lax
from jax.experimental import pallas as pl
from jax.experimental.pallas import tpu as pltpu
from jax.sharding import PartitionSpec as P

HEADS = 24
HEAD_DIM = 128
LOCAL_HEADS = 6
BLOCK = 128
BLOCKS = 64
CHIPS = 16
EPS = 1e-06
TO_LOG2 = HEAD_DIM ** (-0.5) * math.log2(math.e)
LOW = -1e30
VMEM_BYTES = 16 * 1024 * 1024


def attend_body(pieces, first, emit, last, *refs):
    refs = list(refs)
    meta, q_ref = refs.pop(0), refs.pop(0)
    pieces_in = [refs.pop(0) for _ in pieces]
    if not first:
        del refs[:3]
    acc_ref, sum_ref, max_ref = refs.pop(0), refs.pop(0), refs.pop(0)
    if last:
        pack_ref = refs.pop(0)
    if emit:
        buf = refs.pop(0)
        table, sems = refs
    elif last:
        buf, table, sems, level_rows = refs
    else:
        buf, table, sems = refs

    frame = meta[4, 0]
    chip = frame // 2
    core = frame % 2
    copies = []
    places = []
    for number, (chunks, ref) in enumerate(zip(pieces, pieces_in)):
        to = buf.at[pl.ds(len(places) * 256, ref.shape[0])]
        copies.append(pltpu.make_async_copy(ref, to, sems.at[number]))
        for how, distance in chunks:
            source = lax.rem(chip - (1 - 2 * core) * distance + CHIPS, CHIPS)
            low = (2 * source, 2 * source + 1)
            high = (BLOCKS - 1 - 2 * source, BLOCKS - 2 - 2 * source)
            if how == "own":
                places.append((frame, BLOCKS - 1 - frame))
            elif how == "whole":
                places += [low, high]
            else:
                places.append(tuple(jnp.where(core == 0, one, other) for one, other in zip(low, high)))

    for copy in copies:
        copy.start()

    counts = []
    for slot in range(4):
        count = jnp.int32(0)
        for number, (place_a, place_b) in enumerate(places):
            live_a, live_b = meta[slot, place_a], meta[slot, place_b]
            at = 4 * count + slot
            table[at, 0], table[at, 1], table[at, 2] = jnp.int32(number), live_a, live_b
            count = count + jnp.where(live_a + live_b > 0, 1, 0)
        counts.append(count)
        for extra in range(2):
            at = 4 * (count + extra) + slot
            table[at, 0], table[at, 1], table[at, 2] = jnp.int32(0), jnp.int32(0), jnp.int32(0)
    if first:
        acc_ref[...] = jnp.zeros_like(acc_ref)
        sum_ref[...] = jnp.zeros_like(sum_ref)
        max_ref[...] = jnp.full_like(max_ref, LOW)
    for copy in copies:
        copy.wait()

    span = lax.broadcasted_iota(jnp.int32, (1, 256), 1) < BLOCK
    abreast = min(sum(len(chunks) for chunks in pieces), len(places))
    ones = jnp.ones((256 * abreast, HEAD_DIM), jnp.bfloat16)

    def low_if_dead(live):
        return jnp.where(live > 0, 0.0, LOW).astype(jnp.float32)

    def per_slot(slot, carry):
        rows = pl.ds(pl.multiple_of(slot * BLOCK, BLOCK), BLOCK)
        heads = [slice(head * HEAD_DIM, (head + 1) * HEAD_DIM) for head in range(LOCAL_HEADS)]
        count = jnp.where(
            slot < 2,
            jnp.where(slot == 0, counts[0], counts[1]),
            jnp.where(slot == 2, counts[2], counts[3]),
        )

        def per_tiles(index, carry):
            keys_in, values_in, bias_in = [], [], []
            for tile in range(abreast):
                at = 4 * (abreast * index + tile) + slot
                tile_rows = pl.ds(pl.multiple_of(table[at, 0] * 256, 256), 256)
                keys_in.append(buf[tile_rows, :HEAD_DIM])
                values_in.append(buf[tile_rows, HEAD_DIM:])
                bias_in.append(jnp.where(span, low_if_dead(table[at, 1]), low_if_dead(table[at, 2])))
            keys = jnp.concatenate(keys_in, axis=0)
            values = jnp.concatenate([jnp.concatenate(values_in, axis=0), ones], axis=1)
            bias = jnp.concatenate(bias_in, axis=1)
            before = [(max_ref[rows, cols], acc_ref[rows, cols], sum_ref[rows, cols]) for cols in heads]
            scores_of = [
                lax.dot_general(
                    q_ref[rows, cols], keys, (((1,), (1,)), ((), ())), preferred_element_type=jnp.float32
                )
                for cols in heads
            ]
            results = []
            for scores, (prior, acc, total) in zip(scores_of, before):
                scores = scores + bias
                now = jnp.maximum(prior, jnp.max(scores, axis=1, keepdims=True))
                top = now * TO_LOG2
                weights = jnp.exp2(scores * TO_LOG2 - jnp.concatenate([top] * (2 * abreast), axis=1))
                shrink = jnp.exp2(prior * TO_LOG2 - top)
                added = jnp.dot(
                    weights.astype(jnp.bfloat16), values, preferred_element_type=jnp.float32
                )
                results.append(
                    (now, acc * shrink + added[:, :HEAD_DIM], total * shrink + added[:, HEAD_DIM:])
                )
            for cols, (now, acc, total) in zip(heads, results):
                max_ref[rows, cols], acc_ref[rows, cols], sum_ref[rows, cols] = now, acc, total
            return carry

        lax.fori_loop(0, (count + abreast - 1) // abreast, per_tiles, 0)
        return carry

    lax.fori_loop(0, 4, per_slot, 0)

    if last:
        eye = diagonal()
        for slot in range(2):
            rows = slice((2 + slot) * BLOCK, (3 + slot) * BLOCK)
            to = slice(slot * BLOCK, (slot + 1) * BLOCK)
            for head in range(LOCAL_HEADS):
                cols = slice(head * HEAD_DIM, (head + 1) * HEAD_DIM)
                total = jnp.maximum(sum_ref[rows, cols], 1e-30)
                pack_ref[to, cols] = (acc_ref[rows, cols] / total).astype(jnp.bfloat16)
                level = max_ref[rows, cols] * TO_LOG2 + jnp.log2(total)
                level = jnp.sum(jnp.where(eye, level, 0.0), axis=0, keepdims=True)
                parts = []
                for _ in range(3):
                    part = level.astype(jnp.bfloat16).astype(jnp.float32)
                    level = level - part
                    parts.append(part)
                parts.append(jnp.zeros((5, HEAD_DIM), jnp.float32))
                level_rows[8 * slot : 8 * slot + 8, cols] = jnp.concatenate(parts, axis=0)
        pack_ref[2 * BLOCK :, :] = level_rows[...].astype(jnp.bfloat16)


def diagonal():
    return lax.broadcasted_iota(jnp.int32, (BLOCK, BLOCK), 0) == lax.broadcasted_iota(
        jnp.int32, (BLOCK, BLOCK), 1
    )


def attend(pieces, arrays, meta, queries, state, emit=False, last=False):
    first = state is None
    tiles = sum(array.shape[0] // 256 for array in arrays)
    rows, cols = queries.shape
    wide = jax.ShapeDtypeStruct((rows, cols), jnp.float32)
    vmem, smem, anywhere = (
        pl.BlockSpec(memory_space=pltpu.VMEM),
        pl.BlockSpec(memory_space=pltpu.SMEM),
        pl.BlockSpec(memory_space=pl.ANY),
    )
    operands = [meta, queries, *arrays]
    in_specs = [smem, vmem] + [anywhere] * len(arrays)
    scratch = [
        pltpu.VMEM((tiles * 256, 256), jnp.bfloat16),
        pltpu.SMEM((4 * tiles + 16, 4), jnp.int32),
        pltpu.SemaphoreType.DMA((len(arrays),)),
    ]
    aliases = {}
    if not first:
        aliases = {len(operands) + number: number for number in range(3)}
        operands += list(state)
        in_specs += [vmem] * 3
    out_shape = [wide] * 3
    if emit:
        out_shape.append(jax.ShapeDtypeStruct((tiles * 256, 256), jnp.bfloat16))
        scratch = scratch[1:]
    if last:
        out_shape.append(jax.ShapeDtypeStruct((rows // 2 + 16, cols), jnp.bfloat16))
        scratch.append(pltpu.VMEM((16, cols), jnp.float32))
    pairs = tiles * 4 * LOCAL_HEADS
    return pl.pallas_call(
        functools.partial(attend_body, pieces, first, emit, last),
        out_shape=out_shape,
        in_specs=in_specs,
        out_specs=[vmem] * len(out_shape),
        scratch_shapes=scratch,
        input_output_aliases=aliases,
        compiler_params=pltpu.CompilerParams(vmem_limit_bytes=VMEM_BYTES),
        cost_estimate=pl.CostEstimate(
            flops=pairs * 4 * BLOCK * 256 * HEAD_DIM,
            bytes_accessed=8 * rows * cols * 4,
            transcendentals=pairs * BLOCK * 256,
        ),
    )(*operands)


def finish_body(frame_ref, ids_ref, gate_ref, acc_ref, sum_ref, max_ref, theirs, gated_ref, square_ref):
    frame = frame_ref[4, 0]
    places = (frame, BLOCKS - 1 - frame)
    eye = diagonal()
    for slot in range(2):
        rows = slice(slot * BLOCK, (slot + 1) * BLOCK)
        gate_row = gate_ref[pl.ds(ids_ref[places[slot]], 1), :]
        parts = theirs[2 * BLOCK + 8 * slot : 2 * BLOCK + 8 * slot + 8, :].astype(jnp.float32)
        levels = parts[0:1] + parts[1:2] + parts[2:3]
        total = jnp.zeros((BLOCK, HEAD_DIM), jnp.float32)
        for head in range(LOCAL_HEADS):
            cols = slice(head * HEAD_DIM, (head + 1) * HEAD_DIM)
            level = jnp.sum(jnp.where(eye, levels[:, cols], 0.0), axis=1, keepdims=True)
            prior = max_ref[rows, cols] * TO_LOG2
            top = jnp.maximum(prior, level)
            mine, yours = jnp.exp2(prior - top), jnp.exp2(level - top)
            joined = acc_ref[rows, cols] * mine + theirs[rows, cols].astype(jnp.float32) * yours
            gated = joined / (sum_ref[rows, cols] * mine + yours) * gate_row[:, cols]
            gated_ref[rows, cols] = gated
            total = total + gated * gated
        row_total = jnp.sum(total, axis=1, keepdims=True)
        square_ref[slot : slot + 1, :] = jnp.sum(jnp.where(eye, row_total, 0.0), axis=0, keepdims=True)


def finish(meta, section_ids, section_gate, state, theirs):
    cols = theirs.shape[1]
    vmem, smem = pl.BlockSpec(memory_space=pltpu.VMEM), pl.BlockSpec(memory_space=pltpu.SMEM)
    return pl.pallas_call(
        finish_body,
        out_shape=[
            jax.ShapeDtypeStruct((2 * BLOCK, cols), jnp.float32),
            jax.ShapeDtypeStruct((2, BLOCK), jnp.float32),
        ],
        in_specs=[smem, smem] + [vmem] * 5,
        out_specs=[vmem, vmem],
        compiler_params=pltpu.CompilerParams(vmem_limit_bytes=VMEM_BYTES),
    )(meta, section_ids, section_gate, *state, theirs)


def pack_body(keys_ref, values_ref, queries_ref, out_ref, sems):
    copies = []
    at = 0
    for number, ref in enumerate((keys_ref, values_ref, queries_ref)):
        to = out_ref.at[:, at : at + ref.shape[1]]
        copies.append(pltpu.make_async_copy(ref, to, sems.at[number]))
        at += ref.shape[1]
    for copy in copies:
        copy.start()
    for copy in copies:
        copy.wait()


def pack(keys, values, queries):
    anywhere = pl.BlockSpec(memory_space=pltpu.HBM)
    cols = keys.shape[1] + values.shape[1] + queries.shape[1]
    return pl.pallas_call(
        pack_body,
        out_shape=jax.ShapeDtypeStruct((keys.shape[0], cols), keys.dtype),
        in_specs=[anywhere] * 3,
        out_specs=pl.BlockSpec(memory_space=pltpu.VMEM),
        scratch_shapes=[pltpu.SemaphoreType.DMA((3,))],
        compiler_params=pltpu.CompilerParams(vmem_limit_bytes=VMEM_BYTES),
    )(keys, values, queries)


def gather_pair_body(frame_ref, own_ref, other_ref, chunk_ref, both_ref, mine_ref, sems):
    core = frame_ref[0] % 2
    copies = [
        pltpu.make_async_copy(own_ref.at[:, 256:], both_ref.at[0:256], sems.at[0]),
        pltpu.make_async_copy(other_ref.at[:, 256:], both_ref.at[256:512], sems.at[1]),
        pltpu.make_async_copy(own_ref.at[:, :256], mine_ref, sems.at[2]),
    ]
    for half in range(2):
        rows = slice(half * BLOCK, (half + 1) * BLOCK)
        for number, (ref, place) in enumerate(((own_ref, core), (other_ref, 1 - core))):
            to = chunk_ref.at[pl.ds(pl.multiple_of(256 * half + BLOCK * place, BLOCK), BLOCK)]
            copies.append(
                pltpu.make_async_copy(ref.at[rows, :256], to, sems.at[3 + 2 * half + number])
            )
    for copy in copies:
        copy.start()
    for copy in copies:
        copy.wait()


def gather_pair(frame, own, other):
    rows, cols = own.shape
    vmem = pl.BlockSpec(memory_space=pltpu.VMEM)
    return pl.pallas_call(
        gather_pair_body,
        out_shape=[
            jax.ShapeDtypeStruct((2 * rows, 256), own.dtype),
            jax.ShapeDtypeStruct((2 * rows, cols - 256), own.dtype),
            jax.ShapeDtypeStruct((rows, 256), own.dtype),
        ],
        in_specs=[pl.BlockSpec(memory_space=pltpu.SMEM), vmem, vmem],
        out_specs=[vmem] * 3,
        scratch_shapes=[pltpu.SemaphoreType.DMA((7,))],
        compiler_params=pltpu.CompilerParams(vmem_limit_bytes=VMEM_BYTES),
    )(frame, own, other)


def half_body(which, frame_ref, chunk_ref, out_ref, sem):
    rows = out_ref.shape[0]
    part = frame_ref[0] % 2 if which is None else jnp.int32(which)
    at = pl.multiple_of(rows * part, rows)
    copy = pltpu.make_async_copy(chunk_ref.at[pl.ds(at, rows)], out_ref, sem)
    copy.start()
    copy.wait()


def half_of(frame, array, which=None):
    rows, cols = array.shape
    vmem = pl.BlockSpec(memory_space=pltpu.VMEM)
    return pl.pallas_call(
        functools.partial(half_body, which),
        out_shape=jax.ShapeDtypeStruct((rows // 2, cols), array.dtype),
        in_specs=[pl.BlockSpec(memory_space=pltpu.SMEM), vmem],
        out_specs=vmem,
        scratch_shapes=[pltpu.SemaphoreType.DMA],
        compiler_params=pltpu.CompilerParams(vmem_limit_bytes=VMEM_BYTES),
    )(frame, array)


def scale_body(gated_ref, square_ref, gain_ref, out_ref):
    eye = lax.broadcasted_iota(jnp.int32, (BLOCK, BLOCK), 0) == lax.broadcasted_iota(
        jnp.int32, (BLOCK, BLOCK), 1
    )
    for slot in range(2):
        rows = slice(slot * BLOCK, (slot + 1) * BLOCK)
        scale = lax.rsqrt(square_ref[slot : slot + 1, :] / (HEADS * HEAD_DIM) + EPS)
        column = jnp.sum(jnp.where(eye, scale, 0.0), axis=1, keepdims=True)
        out_ref[rows, :] = (gated_ref[rows, :] * column * gain_ref[...]).astype(jnp.bfloat16)


def scale_rows(gated, squares, gain):
    return pl.pallas_call(
        scale_body,
        out_shape=jax.ShapeDtypeStruct(gated.shape, jnp.bfloat16),
        in_specs=[pl.BlockSpec(memory_space=pltpu.VMEM)] * 3,
        out_specs=pl.BlockSpec(memory_space=pltpu.VMEM),
        compiler_params=pltpu.CompilerParams(vmem_limit_bytes=VMEM_BYTES),
    )(gated, squares, gain)


def along(hops):
    return [(2 * z, 2 * ((z + hops) % CHIPS)) for z in range(CHIPS)] + [
        (2 * z + 1, 2 * ((z - hops) % CHIPS) + 1) for z in range(CHIPS)
    ]


def send(array, hops):
    return lax.ppermute(array, "frame", along(hops))


def swap(array):
    return lax.ppermute(array, "frame", [(d, d ^ 1) for d in range(2 * CHIPS)])


def after(array, state):
    array, *state = lax.optimization_barrier((array, *state))
    return array, state


def body(queries, keys, values, block_mask, section_ids, section_gate, norm_gain):
    frame = lax.axis_index("frame")
    here = frame.reshape(1)
    own = pack(keys, values, queries)
    chunk, both, mine = gather_pair(here, own, swap(own))
    places = [frame, BLOCKS - 1 - frame, frame ^ 1, BLOCKS - 1 - (frame ^ 1)]
    meta = jnp.concatenate(
        [lax.dynamic_slice_in_dim(block_mask, place, 1, 0) for place in places]
        + [jnp.full((1, BLOCKS), frame, jnp.int32)],
        axis=0,
    )
    s3 = send(chunk, 3)
    s1 = send(chunk, 1)
    state = attend([[("own", 0)]], [mine], meta, both, None)
    s3, state = after(s3, state)
    s6 = send(s3, 3)
    s4 = send(s3, 1)
    s2 = send(s1, 1)
    state = attend([[("whole", 1)], [("whole", 3)]], [s1, s3], meta, both, state)
    s6, state = after(s6, state)
    s7 = send(s6, 1)
    s8 = send(half_of(here, s6), 2)
    s5 = send(s4, 1)
    state = attend([[("whole", 2)], [("whole", 4)], [("whole", 6)]], [s2, s4, s6], meta, both, state)
    *state, theirs = attend(
        [[("whole", 5)], [("whole", 7)], [("half", 8)]], [s5, s7, s8], meta, both, state, last=True
    )
    gated, squares = finish(meta, section_ids, section_gate, state, swap(theirs))
    squares = lax.psum(squares, "head")
    return scale_rows(gated, squares, norm_gain.reshape(1, -1))


def solution(mesh):
    in_specs = (
        P(("stream", "frame"), "head"),
        P(("stream", "frame"), "head"),
        P(("stream", "frame"), "head"),
        P("stream", None),
        P("stream"),
        P(None, "head"),
        P("head"),
    )
    out_specs = P(("stream", "frame"), "head")
    return jax.shard_map(body, mesh=mesh, in_specs=in_specs, out_specs=out_specs, check_vma=False)
```

time: 101 us -> 84.9 us (0.84)
  starting transfers between devices: 48 us -> 40 us
  waiting for transfers between devices: 12.8 us -> 8.09 us
  Pallas kernels: 24.5 us -> 21.4 us
    ppermute x8, waiting for transfers between devices: 12.3 us -> 4.52 us  [send(): return lax.ppermute(array, 'frame', along(hops))]
    ppermute x4 -> x2, starting transfers between devices: 10.7 us -> 3.84 us  [swap(): return lax.ppermute(array, 'frame', [(d, d ^ 1) for d in range(2 * CHIPS)])]
    ppermute x4 -> x2, waiting for transfers between devices: 0.46 us -> 3.57 us  [swap(): return lax.ppermute(array, 'frame', [(d, d ^ 1) for d in range(2 * CHIPS)])]
    pallas_call x8, Pallas kernels: 23.6 us -> 20.5 us  [the longest x4 18.7 us: attend(): pl.pallas_call(functools.partial(attend_body, pieces, first, emit, last),...]
    unnamed x9 -> x12, local copies, waits for them, and re-layouts: 0.88 us -> 2.69 us
    ppermute x8, starting transfers between devices: 37.3 us -> 36.2 us  [send(): return lax.ppermute(array, 'frame', along(hops))]
  transfers between devices with their start and end apart: 12 -> 10, of which waited for: 5 -> 3; matrix products, arithmetic and copies ran while one was open for 1% -> 1% of each run, Pallas kernels for 14% -> 15%
where the time goes in v2:
time: 84.9 us; the launch traced here: 83.8 us
  starting transfers between devices  40 us (47%)
  Pallas kernels  21.4 us (25%)
  blocking collectives  10.5 us (12%)
  waiting for transfers between devices  8.09 us (10%)
  local copies, waits for them, and re-layouts  3.5 us (4%)
    ppermute x8, starting transfers between devices, send(): return lax.ppermute(array, 'frame', along(hops))  36.2 us
    pallas_call x4, Pallas kernels, attend(): pl.pallas_call(functools.partial(attend_body, pieces, first, emit, last),...  18.7 us
    psum x1, blocking collectives, body(): squares = lax.psum(squares, 'head')  10.5 us
    ppermute x8, waiting for transfers between devices, send(): return lax.ppermute(array, 'frame', along(hops))  4.52 us
    ppermute x2, starting transfers between devices, swap(): return lax.ppermute(array, 'frame', [(d, d ^ 1) for d in range(2 * CHIPS)])  3.84 us
    ppermute x2, waiting for transfers between devices, swap(): return lax.ppermute(array, 'frame', [(d, d ^ 1) for d in range(2 * CHIPS)])  3.57 us
    unnamed x12, local copies, waits for them, and re-layouts  2.69 us
  transfers between devices with their start and end apart: 10, of which 3 were waited for; matrix products, arithmetic and copies ran while one was open for 1% of the time, Pallas kernels for 15%

profile of v2, /device:TPU:24, one launch (start us, length us, event | category | flops | bytes accessed | tf_op | source)
XLA Modules:
  0.0 83.8 jit_solution(15086460274810462124)
XLA Ops:
  0.0 1.0 %copy-done = bf16[256,768]{1,0:T(8,128)(2,1)S(1)} copy-done((bf16[256,768]{1,0:T(8,128)(2,1)S(1)}, bf16[256,768]{1,0:T(8,128)(2,1)}, u32[]{:S(2)}) %copy-start) | copy-done | bytes 393240
  1.0 0.8 copy-done.1
  1.8 0.8 copy-done.2
  2.8 1.9 %collective-permute-start = (bf16[256,1024]{1,0:T(8,128)(2,1)S(1)}, bf16[256,1024]{1,0:T(8,128)(2,1)S(1)}, u32[]{:S(2)}, u32[]{:S(2)}) collective-permute-start(bf16[256,1024]{1,0:T(8,128)(2,1)S(1)} %shard_map.73.own_ref), channel_id=1, source_target_pairs={{0,4},{4,0},{8,12},{12,8},{16,20},{20,16},{24,28},{28,24},{32,36},... | collective-permute-start | bytes 1572872 | tf_op jit(solution)/shard_map/ppermute | solution.py:366
  4.7 1.9 %collective-permute-done.other_ref = bf16[256,1024]{1,0:T(8,128)(2,1)S(1)} collective-permute-done((bf16[256,1024]{1,0:T(8,128)(2,1)S(1)}, bf16[256,1024]{1,0:T(8,128)(2,1)S(1)}, u32[]{:S(2)}, u32[]{:S(2)}) %collective-permute-start) | collective-permute-done | bytes 524320 | tf_op jit(solution)/shard_map/ppermute | solution.py:366
  6.8 6.5 %collective-permute-start.1 = (bf16[512,256]{1,0:T(8,128)(2,1)S(1)}, bf16[512,256]{1,0:T(8,128)(2,1)S(1)}, u32[]{:S(2)}, u32[]{:S(2)}) collective-permute-start(bf16[512,256]{1,0:T(8,128)(2,1)S(1)} %get-tuple-element.32), channel_id=1, source_target_pairs={{0,24},{8,32},{16,40},{24,48},{32,56},{40,64},{48,72},{56,80},{64,... | collective-permute-start | bytes 786440 | tf_op jit(solution)/shard_map/ppermute | solution.py:362
  13.3 5.0 %collective-permute-start.5 = (bf16[512,256]{1,0:T(8,128)(2,1)S(1)}, bf16[512,256]{1,0:T(8,128)(2,1)S(1)}, u32[]{:S(2)}, u32[]{:S(2)}) collective-permute-start(bf16[512,256]{1,0:T(8,128)(2,1)S(1)} %get-tuple-element.32), channel_id=1, source_target_pairs={{0,8},{8,16},{16,24},{24,32},{32,40},{40,48},{48,56},{56,64},{64,7... | collective-permute-start | bytes 786440 | tf_op jit(solution)/shard_map/ppermute | solution.py:362
  18.4 0.8 constant_dynamic-slice_fusion
  19.2 2.3 %shard_map.75 = (f32[512,768]{1,0:T(8,128)S(1)}, f32[512,768]{1,0:T(8,128)S(1)}, f32[512,768]{1,0:T(8,128)S(1)}) custom-call(s32[5,64]{1,0:T(8,128)S(1)} %concatenate.3.refs_0_.frame_ref, bf16[512,768]{1,0:T(8,128)(2,1)S(1)} %get-tuple-element.31.refs_1_, bf16[256,256]{1,0:T(8,128)(2,1)S(1)} %get-tuple-element.33.refs_2_), custom_call_target="tpu_custom_call" | custom-call | flops 402653184 | bytes 12582912 | tf_op jit(solution)/shard_map/pallas_call | solution.py:194
  21.5 4.5 %collective-permute-done.1.refs_3_ = bf16[512,256]{1,0:T(8,128)(2,1)S(1)} collective-permute-done((bf16[512,256]{1,0:T(8,128)(2,1)S(1)}, bf16[512,256]{1,0:T(8,128)(2,1)S(1)}, u32[]{:S(2)}, u32[]{:S(2)}) %collective-permute-start.1) | collective-permute-done | bytes 262176 | tf_op jit(solution)/shard_map/ppermute | solution.py:362
  26.0 4.5 %collective-permute-start.4 = (bf16[512,256]{1,0:T(8,128)(2,1)S(1)}, bf16[512,256]{1,0:T(8,128)(2,1)S(1)}, u32[]{:S(2)}, u32[]{:S(2)}) collective-permute-start(bf16[512,256]{1,0:T(8,128)(2,1)S(1)} %collective-permute-done.1.refs_3_), channel_id=1, source_target_pairs={{0,24},{8,32},{16,40},{24,48},{32,56},{40,64},{48,72},{56,80},{64,... | collective-permute-start | bytes 786440 | tf_op jit(solution)/shard_map/ppermute | solution.py:362
  30.5 3.8 %collective-permute-start.2 = (bf16[512,256]{1,0:T(8,128)(2,1)S(1)}, bf16[512,256]{1,0:T(8,128)(2,1)S(1)}, u32[]{:S(2)}, u32[]{:S(2)}) collective-permute-start(bf16[512,256]{1,0:T(8,128)(2,1)S(1)} %collective-permute-done.1.refs_3_), channel_id=1, source_target_pairs={{0,8},{8,16},{16,24},{24,32},{32,40},{40,48},{48,56},{56,64},{64,7... | collective-permute-start | bytes 786440 | tf_op jit(solution)/shard_map/ppermute | solution.py:362
  34.3 2.9 %collective-permute-start.8 = (bf16[512,256]{1,0:T(8,128)(2,1)S(1)}, bf16[512,256]{1,0:T(8,128)(2,1)S(1)}, u32[]{:S(2)}, u32[]{:S(2)}) collective-permute-start(bf16[512,256]{1,0:T(8,128)(2,1)S(1)} %collective-permute-done.5.refs_2_), channel_id=1, source_target_pairs={{0,8},{8,16},{16,24},{24,32},{32,40},{40,48},{48,56},{56,64},{64,7... | collective-permute-start | bytes 786440 | tf_op jit(solution)/shard_map/ppermute | solution.py:362
  37.2 4.5 %shard_map.76 = (f32[512,768]{1,0:T(8,128)S(1)}, f32[512,768]{1,0:T(8,128)S(1)}, f32[512,768]{1,0:T(8,128)S(1)}) custom-call(s32[5,64]{1,0:T(8,128)S(1)} %concatenate.3.refs_0_.frame_ref, bf16[512,768]{1,0:T(8,128)(2,1)S(1)} %get-tuple-element.31.refs_1_, ...), custom_call_target="tpu_custom_call", output_to_operand_aliasing={{0}: (4, {}), {1}: (5, {}), {2}: (6, {})} | custom-call | flops 1610612736 | bytes 12582912 | tf_op jit(solution)/shard_map/pallas_call | solution.py:194
  41.7 4.9 %collective-permute-start.6 = (bf16[512,256]{1,0:T(8,128)(2,1)S(1)}, bf16[512,256]{1,0:T(8,128)(2,1)S(1)}, u32[]{:S(2)}, u32[]{:S(2)}) collective-permute-start(bf16[512,256]{1,0:T(8,128)(2,1)S(1)} %collective-permute-done.4.chunk_ref.refs_4_), channel_id=1, source_target_pairs={{0,8},{8,16},{16,24},{24,32},{32,40},{40,48},{48,56},{56,64},{64,7... | collective-permute-start | bytes 786440 | tf_op jit(solution)/shard_map/ppermute | solution.py:362
  46.6 3.4 %collective-permute-start.3 = (bf16[512,256]{1,0:T(8,128)(2,1)S(1)}, bf16[512,256]{1,0:T(8,128)(2,1)S(1)}, u32[]{:S(2)}, u32[]{:S(2)}) collective-permute-start(bf16[512,256]{1,0:T(8,128)(2,1)S(1)} %collective-permute-done.2.refs_3_), channel_id=1, source_target_pairs={{0,8},{8,16},{16,24},{24,32},{32,40},{40,48},{48,56},{56,64},{64,7... | collective-permute-start | bytes 786440 | tf_op jit(solution)/shard_map/ppermute | solution.py:362
  50.2 5.2 %collective-permute-start.7 = (bf16[256,256]{1,0:T(8,128)(2,1)S(1)}, bf16[256,256]{1,0:T(8,128)(2,1)S(1)}, u32[]{:S(2)}, u32[]{:S(2)}) collective-permute-start(bf16[256,256]{1,0:T(8,128)(2,1)S(1)} %shard_map.77), channel_id=1, source_target_pairs={{0,16},{8,24},{16,32},{24,40},{32,48},{40,56},{48,64},{56,72},{64,... | collective-permute-start | bytes 393224 | tf_op jit(solution)/shard_map/ppermute | solution.py:362
  55.4 5.7 %shard_map.78 = (f32[512,768]{1,0:T(8,128)S(1)}, f32[512,768]{1,0:T(8,128)S(1)}, f32[512,768]{1,0:T(8,128)S(1)}) custom-call(s32[5,64]{1,0:T(8,128)S(1)} %concatenate.3.refs_0_.frame_ref, bf16[512,768]{1,0:T(8,128)(2,1)S(1)} %get-tuple-element.31.refs_1_, ...), custom_call_target="tpu_custom_call", output_to_operand_aliasing={{0}: (5, {}), {1}: (6, {}), {2}: (7, {})} | custom-call | flops 2415919104 | bytes 12582912 | tf_op jit(solution)/shard_map/pallas_call | solution.py:194
  61.2 6.2 %shard_map.79 = (f32[512,768]{1,0:T(8,128)S(1)}, f32[512,768]{1,0:T(8,128)S(1)}, f32[512,768]{1,0:T(8,128)S(1)}, bf16[272,768]{1,0:T(8,128)(2,1)S(1)}) custom-call(s32[5,64]{1,0:T(8,128)S(1)} %concatenate.3.refs_0_.frame_ref, bf16[512,768]{1,0:T(8,128)(2,1)S(1)} %get-tuple-element.31.refs_1_, ...), custom_call_target="tpu_custom_call", output_to_operand_aliasing={{0}: (5, {}), {1}: (6, {}), {2}: (7, {})} | custom-call | flops 2013265920 | bytes 12582912 | tf_op jit(solution)/shard_map/pallas_call | solution.py:194
  67.4 1.9 %collective-permute-start.9 = (bf16[272,768]{1,0:T(8,128)(2,1)S(1)}, bf16[272,768]{1,0:T(8,128)(2,1)S(1)}, u32[]{:S(2)}, u32[]{:S(2)}) collective-permute-start(bf16[272,768]{1,0:T(8,128)(2,1)S(1)} %get-tuple-element.54), channel_id=1, source_target_pairs={{0,4},{4,0},{8,12},{12,8},{16,20},{20,16},{24,28},{28,24},{32,36},... | collective-permute-start | bytes 1253384 | tf_op jit(solution)/shard_map/ppermute | solution.py:366
  69.4 1.7 %collective-permute-done.9.theirs = bf16[272,768]{1,0:T(8,128)(2,1)S(1)} collective-permute-done((bf16[272,768]{1,0:T(8,128)(2,1)S(1)}, bf16[272,768]{1,0:T(8,128)(2,1)S(1)}, u32[]{:S(2)}, u32[]{:S(2)}) %collective-permute-start.9) | collective-permute-done | bytes 417824 | tf_op jit(solution)/shard_map/ppermute | solution.py:366
  71.1 1.3 %shard_map.80 = (f32[256,768]{1,0:T(8,128)S(1)}, f32[2,128]{1,0:T(2,128)S(1)}) custom-call(s32[5,64]{1,0:T(8,128)S(1)} %concatenate.3.refs_0_.frame_ref, s32[64]{0:T(128)S(1)} %copy-done.4, f32[4,768]{1,0:T(4,128)S(1)} %copy-done.3, f32[512,768]{1,0:T(8,128)S(1)} %get-tuple-element.51.acc_ref, f32[512,768]{1,0:T(8,128)S(1)} %get-tuple-element.52.sum_ref, ...), custom_call_target="tpu_custom_call" | custom-call | tf_op jit(solution)/shard_map/pallas_call | solution.py:237
  72.4 10.5 %psum.7.square_ref = f32[2,128]{1,0:T(2,128)S(1)} all-reduce(f32[2,128]{1,0:T(2,128)S(1)} %get-tuple-element.56), channel_id=1, replica_groups=mesh['stream'=4,'frame'=32,'head'=4] {'head'}, use_global_device_ids=true, to_apply=%region_0.0 | all-reduce | flops 256 | bytes 2048 | tf_op jit(solution)/shard_map/psum | solution.py:402
  82.9 0.9 %shard_map.81 = bf16[256,768]{1,0:T(8,128)(2,1)} custom-call(f32[256,768]{1,0:T(8,128)S(1)} %get-tuple-element.55.gated_ref, f32[2,128]{1,0:T(2,128)S(1)} %psum.7.square_ref, f32[1,768]{1,0:T(1,128)S(1)} %reshape.7.gain_ref), custom_call_target="tpu_custom_call" | custom-call | tf_op jit(solution)/shard_map/pallas_call | solution.py:346
  (22 shorter events, 0.6 us)
Async XLA Ops:
  0.0 1.0 %copy-start = (bf16[256,768]{1,0:T(8,128)(2,1)S(1)}, bf16[256,768]{1,0:T(8,128)(2,1)}, u32[]{:S(2)}) copy-start(bf16[256,768]{1,0:T(8,128)(2,1)} %queries_ref.1) | copy-start | bytes 1179652
  1.0 0.8 %copy-start.1 = (bf16[256,128]{1,0:T(8,128)(2,1)S(1)}, bf16[256,128]{1,0:T(8,128)(2,1)}, u32[]{:S(2)}) copy-start(bf16[256,128]{1,0:T(8,128)(2,1)} %keys_ref.1) | copy-start | bytes 196612
  1.8 0.8 %copy-start.2 = (bf16[256,128]{1,0:T(8,128)(2,1)S(1)}, bf16[256,128]{1,0:T(8,128)(2,1)}, u32[]{:S(2)}) copy-start(bf16[256,128]{1,0:T(8,128)(2,1)} %values_ref.1) | copy-start | bytes 196612
  2.8 3.8 %collective-permute-start = (bf16[256,1024]{1,0:T(8,128)(2,1)S(1)}, bf16[256,1024]{1,0:T(8,128)(2,1)S(1)}, u32[]{:S(2)}, u32[]{:S(2)}) collective-permute-start(bf16[256,1024]{1,0:T(8,128)(2,1)S(1)} %shard_map.73.own_ref), channel_id=1, source_target_pairs={{0,4},{4,0},{8,12},{12,8},{16,20},{20,16},{24,28},{28,24},{32,36},... | collective-permute-start | bytes 1572872 | tf_op jit(solution)/shard_map/ppermute | solution.py:366
  6.8 19.2 %collective-permute-start.1 = (bf16[512,256]{1,0:T(8,128)(2,1)S(1)}, bf16[512,256]{1,0:T(8,128)(2,1)S(1)}, u32[]{:S(2)}, u32[]{:S(2)}) collective-permute-start(bf16[512,256]{1,0:T(8,128)(2,1)S(1)} %get-tuple-element.32), channel_id=1, source_target_pairs={{0,24},{8,32},{16,40},{24,48},{32,56},{40,64},{48,72},{56,80},{64,... | collective-permute-start | bytes 786440 | tf_op jit(solution)/shard_map/ppermute | solution.py:362
  13.3 20.9 %collective-permute-start.5 = (bf16[512,256]{1,0:T(8,128)(2,1)S(1)}, bf16[512,256]{1,0:T(8,128)(2,1)S(1)}, u32[]{:S(2)}, u32[]{:S(2)}) collective-permute-start(bf16[512,256]{1,0:T(8,128)(2,1)S(1)} %get-tuple-element.32), channel_id=1, source_target_pairs={{0,8},{8,16},{16,24},{24,32},{32,40},{40,48},{48,56},{56,64},{64,7... | collective-permute-start | bytes 786440 | tf_op jit(solution)/shard_map/ppermute | solution.py:362
  26.0 15.6 %collective-permute-start.4 = (bf16[512,256]{1,0:T(8,128)(2,1)S(1)}, bf16[512,256]{1,0:T(8,128)(2,1)S(1)}, u32[]{:S(2)}, u32[]{:S(2)}) collective-permute-start(bf16[512,256]{1,0:T(8,128)(2,1)S(1)} %collective-permute-done.1.refs_3_), channel_id=1, source_target_pairs={{0,24},{8,32},{16,40},{24,48},{32,56},{40,64},{48,72},{56,80},{64,... | collective-permute-start | bytes 786440 | tf_op jit(solution)/shard_map/ppermute | solution.py:362
  30.5 16.1 %collective-permute-start.2 = (bf16[512,256]{1,0:T(8,128)(2,1)S(1)}, bf16[512,256]{1,0:T(8,128)(2,1)S(1)}, u32[]{:S(2)}, u32[]{:S(2)}) collective-permute-start(bf16[512,256]{1,0:T(8,128)(2,1)S(1)} %collective-permute-done.1.refs_3_), channel_id=1, source_target_pairs={{0,8},{8,16},{16,24},{24,32},{32,40},{40,48},{48,56},{56,64},{64,7... | collective-permute-start | bytes 786440 | tf_op jit(solution)/shard_map/ppermute | solution.py:362
  34.3 21.1 %collective-permute-start.8 = (bf16[512,256]{1,0:T(8,128)(2,1)S(1)}, bf16[512,256]{1,0:T(8,128)(2,1)S(1)}, u32[]{:S(2)}, u32[]{:S(2)}) collective-permute-start(bf16[512,256]{1,0:T(8,128)(2,1)S(1)} %collective-permute-done.5.refs_2_), channel_id=1, source_target_pairs={{0,8},{8,16},{16,24},{24,32},{32,40},{40,48},{48,56},{56,64},{64,7... | collective-permute-start | bytes 786440 | tf_op jit(solution)/shard_map/ppermute | solution.py:362
  41.7 19.5 %collective-permute-start.6 = (bf16[512,256]{1,0:T(8,128)(2,1)S(1)}, bf16[512,256]{1,0:T(8,128)(2,1)S(1)}, u32[]{:S(2)}, u32[]{:S(2)}) collective-permute-start(bf16[512,256]{1,0:T(8,128)(2,1)S(1)} %collective-permute-done.4.chunk_ref.refs_4_), channel_id=1, source_target_pairs={{0,8},{8,16},{16,24},{24,32},{32,40},{40,48},{48,56},{56,64},{64,7... | collective-permute-start | bytes 786440 | tf_op jit(solution)/shard_map/ppermute | solution.py:362
  46.6 14.6 %collective-permute-start.3 = (bf16[512,256]{1,0:T(8,128)(2,1)S(1)}, bf16[512,256]{1,0:T(8,128)(2,1)S(1)}, u32[]{:S(2)}, u32[]{:S(2)}) collective-permute-start(bf16[512,256]{1,0:T(8,128)(2,1)S(1)} %collective-permute-done.2.refs_3_), channel_id=1, source_target_pairs={{0,8},{8,16},{16,24},{24,32},{32,40},{40,48},{48,56},{56,64},{64,7... | collective-permute-start | bytes 786440 | tf_op jit(solution)/shard_map/ppermute | solution.py:362
  50.2 11.0 %collective-permute-start.7 = (bf16[256,256]{1,0:T(8,128)(2,1)S(1)}, bf16[256,256]{1,0:T(8,128)(2,1)S(1)}, u32[]{:S(2)}, u32[]{:S(2)}) collective-permute-start(bf16[256,256]{1,0:T(8,128)(2,1)S(1)} %shard_map.77), channel_id=1, source_target_pairs={{0,16},{8,24},{16,32},{24,40},{32,48},{40,56},{48,64},{56,72},{64,... | collective-permute-start | bytes 393224 | tf_op jit(solution)/shard_map/ppermute | solution.py:362
  61.2 8.2 %copy-start.5 = (f32[768]{0:T(1024)S(1)}, f32[768]{0:T(1024)}, u32[]{:S(2)}) copy-start(f32[768]{0:T(1024)} %param.13) | copy-start | bytes 9220
  61.2 9.9 %copy-start.3 = (f32[4,768]{1,0:T(4,128)S(1)}, f32[4,768]{1,0:T(4,128)}, u32[]{:S(2)}) copy-start(f32[4,768]{1,0:T(4,128)} %gate_ref.1) | copy-start | bytes 36868
  61.2 9.9 %copy-start.4 = (s32[64]{0:T(128)S(1)}, s32[64]{0:T(128)}, u32[]{:S(2)}) copy-start(s32[64]{0:T(128)} %ids_ref.1) | copy-start | bytes 772
  67.4 3.7 %collective-permute-start.9 = (bf16[272,768]{1,0:T(8,128)(2,1)S(1)}, bf16[272,768]{1,0:T(8,128)(2,1)S(1)}, u32[]{:S(2)}, u32[]{:S(2)}) collective-permute-start(bf16[272,768]{1,0:T(8,128)(2,1)S(1)} %get-tuple-element.54), channel_id=1, source_target_pairs={{0,4},{4,0},{8,12},{12,8},{16,20},{20,16},{24,28},{28,24},{32,36},... | collective-permute-start | bytes 1253384 | tf_op jit(solution)/shard_map/ppermute | solution.py:366

commit v3 on v2

--- a/solution.py
+++ b/solution.py
@@ -20,119 +20,90 @@
 VMEM_BYTES = 16 * 1024 * 1024
 
 
-def attend_body(pieces, first, emit, last, *refs):
+def attend_body(pieces, first, last, *refs):
     refs = list(refs)
     meta, q_ref = refs.pop(0), refs.pop(0)
-    pieces_in = [refs.pop(0) for _ in pieces]
+    arrays = [refs.pop(0) for _ in pieces]
     if not first:
         del refs[:3]
     acc_ref, sum_ref, max_ref = refs.pop(0), refs.pop(0), refs.pop(0)
     if last:
-        pack_ref = refs.pop(0)
-    if emit:
-        buf = refs.pop(0)
-        table, sems = refs
-    elif last:
-        buf, table, sems, level_rows = refs
-    else:
-        buf, table, sems = refs
+        pack_ref, level_rows = refs
 
     frame = meta[4, 0]
     chip = frame // 2
     core = frame % 2
-    copies = []
-    places = []
-    for number, (chunks, ref) in enumerate(zip(pieces, pieces_in)):
-        to = buf.at[pl.ds(len(places) * 256, ref.shape[0])]
-        copies.append(pltpu.make_async_copy(ref, to, sems.at[number]))
-        for how, distance in chunks:
-            source = lax.rem(chip - (1 - 2 * core) * distance + CHIPS, CHIPS)
-            low = (2 * source, 2 * source + 1)
-            high = (BLOCKS - 1 - 2 * source, BLOCKS - 2 - 2 * source)
-            if how == "own":
-                places.append((frame, BLOCKS - 1 - frame))
-            elif how == "whole":
-                places += [low, high]
-            else:
-                places.append(tuple(jnp.where(core == 0, one, other) for one, other in zip(low, high)))
-
-    for copy in copies:
-        copy.start()
-
-    counts = []
-    for slot in range(4):
-        count = jnp.int32(0)
-        for number, (place_a, place_b) in enumerate(places):
-            live_a, live_b = meta[slot, place_a], meta[slot, place_b]
-            at = 4 * count + slot
-            table[at, 0], table[at, 1], table[at, 2] = jnp.int32(number), live_a, live_b
-            count = count + jnp.where(live_a + live_b > 0, 1, 0)
-        counts.append(count)
-        for extra in range(2):
-            at = 4 * (count + extra) + slot
-            table[at, 0], table[at, 1], table[at, 2] = jnp.int32(0), jnp.int32(0), jnp.int32(0)
+    groups = [[], []]
+    for ref, (how, distance) in zip(arrays, pieces):
+        source = lax.rem(chip - (1 - 2 * core) * distance + CHIPS, CHIPS)
+        low = (2 * source, 2 * source + 1)
+        high = (BLOCKS - 1 - 2 * source, BLOCKS - 2 - 2 * source)
+        if how == "own":
+            groups[0].append((ref, slice(0, 256), (frame, BLOCKS - 1 - frame)))
+        elif how == "whole":
+            groups[0].append((ref, slice(0, 256), low))
+            groups[1].append((ref, slice(256, 512), high))
+        else:
+            places = tuple(jnp.where(core == 0, one, other) for one, other in zip(low, high))
+            groups[0].append((ref, slice(0, 256), places))
     if first:
         acc_ref[...] = jnp.zeros_like(acc_ref)
         sum_ref[...] = jnp.zeros_like(sum_ref)
         max_ref[...] = jnp.full_like(max_ref, LOW)
-    for copy in copies:
-        copy.wait()
-
-    span = lax.broadcasted_iota(jnp.int32, (1, 256), 1) < BLOCK
-    abreast = min(sum(len(chunks) for chunks in pieces), len(places))
-    ones = jnp.ones((256 * abreast, HEAD_DIM), jnp.bfloat16)
-
-    def low_if_dead(live):
-        return jnp.where(live > 0, 0.0, LOW).astype(jnp.float32)
-
-    def per_slot(slot, carry):
+    heads = [slice(head * HEAD_DIM, (head + 1) * HEAD_DIM) for head in range(LOCAL_HEADS)]
+
+    def add(tiles, slot, lives):
         rows = pl.ds(pl.multiple_of(slot * BLOCK, BLOCK), BLOCK)
-        heads = [slice(head * HEAD_DIM, (head + 1) * HEAD_DIM) for head in range(LOCAL_HEADS)]
-        count = jnp.where(
-            slot < 2,
-            jnp.where(slot == 0, counts[0], counts[1]),
-            jnp.where(slot == 2, counts[2], counts[3]),
-        )
-
-        def per_tiles(index, carry):
-            keys_in, values_in, bias_in = [], [], []
-            for tile in range(abreast):
-                at = 4 * (abreast * index + tile) + slot
-                tile_rows = pl.ds(pl.multiple_of(table[at, 0] * 256, 256), 256)
-                keys_in.append(buf[tile_rows, :HEAD_DIM])
-                values_in.append(buf[tile_rows, HEAD_DIM:])
-                bias_in.append(jnp.where(span, low_if_dead(table[at, 1]), low_if_dead(table[at, 2])))
-            keys = jnp.concatenate(keys_in, axis=0)
-            values = jnp.concatenate([jnp.concatenate(values_in, axis=0), ones], axis=1)
-            bias = jnp.concatenate(bias_in, axis=1)
-            before = [(max_ref[rows, cols], acc_ref[rows, cols], sum_ref[rows, cols]) for cols in heads]
-            scores_of = [
-                lax.dot_general(
-                    q_ref[rows, cols], keys, (((1,), (1,)), ((), ())), preferred_element_type=jnp.float32
-                )
-                for cols in heads
-            ]
-            results = []
-            for scores, (prior, acc, total) in zip(scores_of, before):
-                scores = scores + bias
-                now = jnp.maximum(prior, jnp.max(scores, axis=1, keepdims=True))
-                top = now * TO_LOG2
-                weights = jnp.exp2(scores * TO_LOG2 - jnp.concatenate([top] * (2 * abreast), axis=1))
-                shrink = jnp.exp2(prior * TO_LOG2 - top)
-                added = jnp.dot(
-                    weights.astype(jnp.bfloat16), values, preferred_element_type=jnp.float32
-                )
-                results.append(
-                    (now, acc * shrink + added[:, :HEAD_DIM], total * shrink + added[:, HEAD_DIM:])
-                )
-            for cols, (now, acc, total) in zip(heads, results):
-                max_ref[rows, cols], acc_ref[rows, cols], sum_ref[rows, cols] = now, acc, total
+        width = 256 * len(tiles)
+        keys = jnp.concatenate([ref[at, :HEAD_DIM] for ref, at, _ in tiles], axis=0)
+        values = jnp.concatenate([ref[at, HEAD_DIM:] for ref, at, _ in tiles], axis=0)
+        values = jnp.concatenate([values, jnp.ones((width, HEAD_DIM), jnp.bfloat16)], axis=1)
+        before = [(max_ref[rows, cols], acc_ref[rows, cols], sum_ref[rows, cols]) for cols in heads]
+        scores_of = [
+            lax.dot_general(
+                q_ref[rows, cols], keys, (((1,), (1,)), ((), ())), preferred_element_type=jnp.float32
+            )
+            for cols in heads
+        ]
+        if lives is not None:
+            bias = jnp.concatenate(
+                [
+                    jnp.broadcast_to(jnp.where(live > 0, 0.0, LOW).astype(jnp.float32), (1, BLOCK))
+                    for live in lives
+                ],
+                axis=1,
+            )
+            scores_of = [scores + bias for scores in scores_of]
+        results = []
+        for scores, (prior, acc, total) in zip(scores_of, before):
+            now = jnp.maximum(prior, jnp.max(scores, axis=1, keepdims=True))
+            top = now * TO_LOG2
+            weights = jnp.exp2(scores * TO_LOG2 - jnp.concatenate([top] * (width // BLOCK), axis=1))
+            shrink = jnp.exp2(prior * TO_LOG2 - top)
+            added = jnp.dot(weights.astype(jnp.bfloat16), values, preferred_element_type=jnp.float32)
+            results.append((now, acc * shrink + added[:, :HEAD_DIM], total * shrink + added[:, HEAD_DIM:]))
+        for cols, (now, acc, total) in zip(heads, results):
+            max_ref[rows, cols], acc_ref[rows, cols], sum_ref[rows, cols] = now, acc, total
+
+    for tiles in groups:
+        if not tiles:
+            continue
+
+        def per_slot(slot, carry, tiles=tiles):
+            lives = [meta[slot, place] for _, _, places in tiles for place in places]
+            count = sum(lives)
+
+            @pl.when(count == len(lives))
+            def _():
+                add(tiles, slot, None)
+
+            @pl.when(jnp.logical_and(count > 0, count < len(lives)))
+            def _():
+                add(tiles, slot, lives)
+
             return carry
 
-        lax.fori_loop(0, (count + abreast - 1) // abreast, per_tiles, 0)
-        return carry
-
-    lax.fori_loop(0, 4, per_slot, 0)
+        lax.fori_loop(0, 4, per_slot, 0)
 
     if last:
         eye = diagonal()
@@ -161,38 +132,26 @@
     )
 
 
-def attend(pieces, arrays, meta, queries, state, emit=False, last=False):
+def attend(pieces, arrays, meta, queries, state, last=False):
     first = state is None
     tiles = sum(array.shape[0] // 256 for array in arrays)
     rows, cols = queries.shape
-    wide = jax.ShapeDtypeStruct((rows, cols), jnp.float32)
-    vmem, smem, anywhere = (
-        pl.BlockSpec(memory_space=pltpu.VMEM),
-        pl.BlockSpec(memory_space=pltpu.SMEM),
-        pl.BlockSpec(memory_space=pl.ANY),
-    )
+    vmem, smem = pl.BlockSpec(memory_space=pltpu.VMEM), pl.BlockSpec(memory_space=pltpu.SMEM)
     operands = [meta, queries, *arrays]
-    in_specs = [smem, vmem] + [anywhere] * len(arrays)
-    scratch = [
-        pltpu.VMEM((tiles * 256, 256), jnp.bfloat16),
-        pltpu.SMEM((4 * tiles + 16, 4), jnp.int32),
-        pltpu.SemaphoreType.DMA((len(arrays),)),
-    ]
+    in_specs = [smem] + [vmem] * (1 + len(arrays))
     aliases = {}
     if not first:
         aliases = {len(operands) + number: number for number in range(3)}
         operands += list(state)
         in_specs += [vmem] * 3
-    out_shape = [wide] * 3
-    if emit:
-        out_shape.append(jax.ShapeDtypeStruct((tiles * 256, 256), jnp.bfloat16))
-        scratch = scratch[1:]
+    out_shape = [jax.ShapeDtypeStruct((rows, cols), jnp.float32)] * 3
+    scratch = []
     if last:
         out_shape.append(jax.ShapeDtypeStruct((rows // 2 + 16, cols), jnp.bfloat16))
         scratch.append(pltpu.VMEM((16, cols), jnp.float32))
     pairs = tiles * 4 * LOCAL_HEADS
     return pl.pallas_call(
-        functools.partial(attend_body, pieces, first, emit, last),
+        functools.partial(attend_body, pieces, first, last),
         out_shape=out_shape,
         in_specs=in_specs,
         out_specs=[vmem] * len(out_shape),
@@ -269,7 +228,7 @@
         out_specs=pl.BlockSpec(memory_space=pltpu.VMEM),
         scratch_shapes=[pltpu.SemaphoreType.DMA((3,))],
         compiler_params=pltpu.CompilerParams(vmem_limit_bytes=VMEM_BYTES),
-    )(keys, values, queries)
+    )(*(pltpu.with_memory_space_constraint(array, pltpu.HBM) for array in (keys, values, queries)))
 
 
 def gather_pair_body(frame_ref, own_ref, other_ref, chunk_ref, both_ref, mine_ref, sems):
@@ -337,7 +296,8 @@
     )
     for slot in range(2):
         rows = slice(slot * BLOCK, (slot + 1) * BLOCK)
-        scale = lax.rsqrt(square_ref[slot : slot + 1, :] / (HEADS * HEAD_DIM) + EPS)
+        square = sum(square_ref[part, slot : slot + 1, :] for part in range(square_ref.shape[0]))
+        scale = lax.rsqrt(square / (HEADS * HEAD_DIM) + EPS)
         column = jnp.sum(jnp.where(eye, scale, 0.0), axis=1, keepdims=True)
         out_ref[rows, :] = (gated_ref[rows, :] * column * gain_ref[...]).astype(jnp.bfloat16)
 
@@ -384,22 +344,22 @@
     )
     s3 = send(chunk, 3)
     s1 = send(chunk, 1)
-    state = attend([[("own", 0)]], [mine], meta, both, None)
+    state = attend([("own", 0)], [mine], meta, both, None)
     s3, state = after(s3, state)
     s6 = send(s3, 3)
     s4 = send(s3, 1)
     s2 = send(s1, 1)
-    state = attend([[("whole", 1)], [("whole", 3)]], [s1, s3], meta, both, state)
+    state = attend([("whole", 1), ("whole", 3)], [s1, s3], meta, both, state)
     s6, state = after(s6, state)
     s7 = send(s6, 1)
     s8 = send(half_of(here, s6), 2)
     s5 = send(s4, 1)
-    state = attend([[("whole", 2)], [("whole", 4)], [("whole", 6)]], [s2, s4, s6], meta, both, state)
+    state = attend([("whole", 2), ("whole", 4), ("whole", 6)], [s2, s4, s6], meta, both, state)
     *state, theirs = attend(
-        [[("whole", 5)], [("whole", 7)], [("half", 8)]], [s5, s7, s8], meta, both, state, last=True
+        [("whole", 5), ("whole", 7), ("half", 8)], [s5, s7, s8], meta, both, state, last=True
     )
     gated, squares = finish(meta, section_ids, section_gate, state, swap(theirs))
-    squares = lax.psum(squares, "head")
+    squares = lax.all_gather(squares, "head", axis=0)
     return scale_rows(gated, squares, norm_gain.reshape(1, -1))
 
 

time: 84.9 us -> 80.8 us (0.952)
  the two profiles are of different devices: /device:TPU:24 before, /device:TPU:160 now
where the time goes in v3:
time: 80.8 us; the launch traced here: 80.4 us
  starting transfers between devices  42.4 us (52%)
  Pallas kernels  23 us (28%)
  blocking collectives  8.92 us (11%)
  waiting for transfers between devices  5.07 us (6%)
  local copies, waits for them, and re-layouts  0.83 us (1%)
    ppermute x8, starting transfers between devices, send(): return lax.ppermute(array, 'frame', along(hops))  38.5 us
    pallas_call x4, Pallas kernels, attend(): pl.pallas_call(functools.partial(attend_body, pieces, first, last), out_s...  19.2 us
    all_gather x1, blocking collectives, body(): squares = lax.all_gather(squares, 'head', axis=0)  8.92 us
    ppermute x2, starting transfers between devices, swap(): return lax.ppermute(array, 'frame', [(d, d ^ 1) for d in range(2 * CHIPS)])  3.84 us
    ppermute x2, waiting for transfers between devices, swap(): return lax.ppermute(array, 'frame', [(d, d ^ 1) for d in range(2 * CHIPS)])  3.57 us
  transfers between devices with their start and end apart: 10, of which 3 were waited for; matrix products, arithmetic and copies ran while one was open for 1% of the time, Pallas kernels for 16%

profile of v3, /device:TPU:160, one launch (start us, length us, event | category | flops | bytes accessed | tf_op | source)
XLA Modules:
  0.0 80.4 jit_solution(8614293119749624333)
XLA Ops:
  0.0 1.1 %shard_map.73.own_ref = bf16[256,1024]{1,0:T(8,128)(2,1)S(1)} custom-call(bf16[256,128]{1,0:T(8,128)(2,1)} %keys_ref.1, bf16[256,128]{1,0:T(8,128)(2,1)} %values_ref.1, bf16[256,768]{1,0:T(8,128)(2,1)} %queries_ref.1), custom_call_target="tpu_custom_call" | custom-call | tf_op jit(solution)/shard_map/pallas_call | solution.py:224
  1.1 1.9 %collective-permute-start = (bf16[256,1024]{1,0:T(8,128)(2,1)S(1)}, bf16[256,1024]{1,0:T(8,128)(2,1)S(1)}, u32[]{:S(2)}, u32[]{:S(2)}) collective-permute-start(bf16[256,1024]{1,0:T(8,128)(2,1)S(1)} %shard_map.73.own_ref), channel_id=1, source_target_pairs={{0,4},{4,0},{8,12},{12,8},{16,20},{20,16},{24,28},{28,24},{32,36},... | collective-permute-start | bytes 1572872 | tf_op jit(solution)/shard_map/ppermute | solution.py:326
  3.0 1.9 %collective-permute-done.other_ref = bf16[256,1024]{1,0:T(8,128)(2,1)S(1)} collective-permute-done((bf16[256,1024]{1,0:T(8,128)(2,1)S(1)}, bf16[256,1024]{1,0:T(8,128)(2,1)S(1)}, u32[]{:S(2)}, u32[]{:S(2)}) %collective-permute-start) | collective-permute-done | bytes 524320 | tf_op jit(solution)/shard_map/ppermute | solution.py:326
  4.9 0.2 shard_map.74
  5.1 7.7 %collective-permute-start.1 = (bf16[512,256]{1,0:T(8,128)(2,1)S(1)}, bf16[512,256]{1,0:T(8,128)(2,1)S(1)}, u32[]{:S(2)}, u32[]{:S(2)}) collective-permute-start(bf16[512,256]{1,0:T(8,128)(2,1)S(1)} %get-tuple-element.32), channel_id=1, source_target_pairs={{0,24},{8,32},{16,40},{24,48},{32,56},{40,64},{48,72},{56,80},{64,... | collective-permute-start | bytes 786440 | tf_op jit(solution)/shard_map/ppermute | solution.py:322
  12.9 2.9 %collective-permute-start.5 = (bf16[512,256]{1,0:T(8,128)(2,1)S(1)}, bf16[512,256]{1,0:T(8,128)(2,1)S(1)}, u32[]{:S(2)}, u32[]{:S(2)}) collective-permute-start(bf16[512,256]{1,0:T(8,128)(2,1)S(1)} %get-tuple-element.32), channel_id=1, source_target_pairs={{0,8},{8,16},{16,24},{24,32},{32,40},{40,48},{48,56},{56,64},{64,7... | collective-permute-start | bytes 786440 | tf_op jit(solution)/shard_map/ppermute | solution.py:322
  15.8 0.8 constant_dynamic-slice_fusion
  16.6 2.7 %shard_map.75 = (f32[512,768]{1,0:T(8,128)S(1)}, f32[512,768]{1,0:T(8,128)S(1)}, f32[512,768]{1,0:T(8,128)S(1)}) custom-call(s32[5,64]{1,0:T(8,128)S(1)} %concatenate.3.refs_0_.frame_ref, bf16[512,768]{1,0:T(8,128)(2,1)S(1)} %get-tuple-element.31.refs_1_, bf16[256,256]{1,0:T(8,128)(2,1)S(1)} %get-tuple-element.33.refs_2_), custom_call_target="tpu_custom_call" | custom-call | flops 402653184 | bytes 12582912 | tf_op jit(solution)/shard_map/pallas_call | solution.py:153
  19.4 1.5 %collective-permute-done.1.refs_3_ = bf16[512,256]{1,0:T(8,128)(2,1)S(1)} collective-permute-done((bf16[512,256]{1,0:T(8,128)(2,1)S(1)}, bf16[512,256]{1,0:T(8,128)(2,1)S(1)}, u32[]{:S(2)}, u32[]{:S(2)}) %collective-permute-start.1) | collective-permute-done | bytes 262176 | tf_op jit(solution)/shard_map/ppermute | solution.py:322
  20.9 5.9 %collective-permute-start.4 = (bf16[512,256]{1,0:T(8,128)(2,1)S(1)}, bf16[512,256]{1,0:T(8,128)(2,1)S(1)}, u32[]{:S(2)}, u32[]{:S(2)}) collective-permute-start(bf16[512,256]{1,0:T(8,128)(2,1)S(1)} %collective-permute-done.1.refs_3_), channel_id=1, source_target_pairs={{0,24},{8,32},{16,40},{24,48},{32,56},{40,64},{48,72},{56,80},{64,... | collective-permute-start | bytes 786440 | tf_op jit(solution)/shard_map/ppermute | solution.py:322
  26.8 5.3 %collective-permute-start.2 = (bf16[512,256]{1,0:T(8,128)(2,1)S(1)}, bf16[512,256]{1,0:T(8,128)(2,1)S(1)}, u32[]{:S(2)}, u32[]{:S(2)}) collective-permute-start(bf16[512,256]{1,0:T(8,128)(2,1)S(1)} %collective-permute-done.1.refs_3_), channel_id=1, source_target_pairs={{0,8},{8,16},{16,24},{24,32},{32,40},{40,48},{48,56},{56,64},{64,7... | collective-permute-start | bytes 786440 | tf_op jit(solution)/shard_map/ppermute | solution.py:322
  32.1 3.7 %collective-permute-start.8 = (bf16[512,256]{1,0:T(8,128)(2,1)S(1)}, bf16[512,256]{1,0:T(8,128)(2,1)S(1)}, u32[]{:S(2)}, u32[]{:S(2)}) collective-permute-start(bf16[512,256]{1,0:T(8,128)(2,1)S(1)} %collective-permute-done.5.refs_2_), channel_id=1, source_target_pairs={{0,8},{8,16},{16,24},{24,32},{32,40},{40,48},{48,56},{56,64},{64,7... | collective-permute-start | bytes 786440 | tf_op jit(solution)/shard_map/ppermute | solution.py:322
  35.8 2.5 %shard_map.76 = (f32[512,768]{1,0:T(8,128)S(1)}, f32[512,768]{1,0:T(8,128)S(1)}, f32[512,768]{1,0:T(8,128)S(1)}) custom-call(s32[5,64]{1,0:T(8,128)S(1)} %concatenate.3.refs_0_.frame_ref, bf16[512,768]{1,0:T(8,128)(2,1)S(1)} %get-tuple-element.31.refs_1_, ...), custom_call_target="tpu_custom_call", output_to_operand_aliasing={{0}: (4, {}), {1}: (5, {}), {2}: (6, {})} | custom-call | flops 1610612736 | bytes 12582912 | tf_op jit(solution)/shard_map/pallas_call | solution.py:153
  38.4 4.2 %collective-permute-start.6 = (bf16[512,256]{1,0:T(8,128)(2,1)S(1)}, bf16[512,256]{1,0:T(8,128)(2,1)S(1)}, u32[]{:S(2)}, u32[]{:S(2)}) collective-permute-start(bf16[512,256]{1,0:T(8,128)(2,1)S(1)} %collective-permute-done.4.chunk_ref.refs_4_), channel_id=1, source_target_pairs={{0,8},{8,16},{16,24},{24,32},{32,40},{40,48},{48,56},{56,64},{64,7... | collective-permute-start | bytes 786440 | tf_op jit(solution)/shard_map/ppermute | solution.py:322
  42.5 2.7 %collective-permute-start.3 = (bf16[512,256]{1,0:T(8,128)(2,1)S(1)}, bf16[512,256]{1,0:T(8,128)(2,1)S(1)}, u32[]{:S(2)}, u32[]{:S(2)}) collective-permute-start(bf16[512,256]{1,0:T(8,128)(2,1)S(1)} %collective-permute-done.2.refs_3_), channel_id=1, source_target_pairs={{0,8},{8,16},{16,24},{24,32},{32,40},{40,48},{48,56},{56,64},{64,7... | collective-permute-start | bytes 786440 | tf_op jit(solution)/shard_map/ppermute | solution.py:322
  45.2 0.2 shard_map.77
  45.4 6.1 %collective-permute-start.7 = (bf16[256,256]{1,0:T(8,128)(2,1)S(1)}, bf16[256,256]{1,0:T(8,128)(2,1)S(1)}, u32[]{:S(2)}, u32[]{:S(2)}) collective-permute-start(bf16[256,256]{1,0:T(8,128)(2,1)S(1)} %shard_map.77), channel_id=1, source_target_pairs={{0,16},{8,24},{16,32},{24,40},{32,48},{40,56},{48,64},{56,72},{64,... | collective-permute-start | bytes 393224 | tf_op jit(solution)/shard_map/ppermute | solution.py:322
  51.5 7.7 %shard_map.78 = (f32[512,768]{1,0:T(8,128)S(1)}, f32[512,768]{1,0:T(8,128)S(1)}, f32[512,768]{1,0:T(8,128)S(1)}) custom-call(s32[5,64]{1,0:T(8,128)S(1)} %concatenate.3.refs_0_.frame_ref, bf16[512,768]{1,0:T(8,128)(2,1)S(1)} %get-tuple-element.31.refs_1_, ...), custom_call_target="tpu_custom_call", output_to_operand_aliasing={{0}: (5, {}), {1}: (6, {}), {2}: (7, {})} | custom-call | flops 2415919104 | bytes 12582912 | tf_op jit(solution)/shard_map/pallas_call | solution.py:153
  59.3 6.3 %shard_map.79 = (f32[512,768]{1,0:T(8,128)S(1)}, f32[512,768]{1,0:T(8,128)S(1)}, f32[512,768]{1,0:T(8,128)S(1)}, bf16[272,768]{1,0:T(8,128)(2,1)S(1)}) custom-call(s32[5,64]{1,0:T(8,128)S(1)} %concatenate.3.refs_0_.frame_ref, bf16[512,768]{1,0:T(8,128)(2,1)S(1)} %get-tuple-element.31.refs_1_, ...), custom_call_target="tpu_custom_call", output_to_operand_aliasing={{0}: (5, {}), {1}: (6, {}), {2}: (7, {})} | custom-call | flops 2013265920 | bytes 12582912 | tf_op jit(solution)/shard_map/pallas_call | solution.py:153
  65.6 1.9 %collective-permute-start.9 = (bf16[272,768]{1,0:T(8,128)(2,1)S(1)}, bf16[272,768]{1,0:T(8,128)(2,1)S(1)}, u32[]{:S(2)}, u32[]{:S(2)}) collective-permute-start(bf16[272,768]{1,0:T(8,128)(2,1)S(1)} %get-tuple-element.54), channel_id=1, source_target_pairs={{0,4},{4,0},{8,12},{12,8},{16,20},{20,16},{24,28},{28,24},{32,36},... | collective-permute-start | bytes 1253384 | tf_op jit(solution)/shard_map/ppermute | solution.py:326
  67.6 1.7 %collective-permute-done.9.theirs = bf16[272,768]{1,0:T(8,128)(2,1)S(1)} collective-permute-done((bf16[272,768]{1,0:T(8,128)(2,1)S(1)}, bf16[272,768]{1,0:T(8,128)(2,1)S(1)}, u32[]{:S(2)}, u32[]{:S(2)}) %collective-permute-start.9) | collective-permute-done | bytes 417824 | tf_op jit(solution)/shard_map/ppermute | solution.py:326
  69.3 1.3 %shard_map.80 = (f32[256,768]{1,0:T(8,128)S(1)}, f32[2,128]{1,0:T(2,128)S(1)}) custom-call(s32[5,64]{1,0:T(8,128)S(1)} %concatenate.3.refs_0_.frame_ref, s32[64]{0:T(128)S(1)} %copy-done.1, f32[4,768]{1,0:T(4,128)S(1)} %copy-done, f32[512,768]{1,0:T(8,128)S(1)} %get-tuple-element.51.acc_ref, f32[512,768]{1,0:T(8,128)S(1)} %get-tuple-element.52.sum_ref, ...), custom_call_target="tpu_custom_call" | custom-call | tf_op jit(solution)/shard_map/pallas_call | solution.py:196
  70.6 8.9 %all-gather.1.square_ref = f32[4,2,128]{2,1,0:T(2,128)S(1)} all-gather(f32[1,2,128]{2,1,0:T(2,128)S(1)} %bitcast.2), channel_id=2, replica_groups=mesh['stream'=4,'frame'=32,'head'=4] {'head'}, dimensions={0}, use_global_device_ids=true | all-gather | bytes 5120 | tf_op jit(solution)/shard_map/all_gather | solution.py:362
  79.5 0.9 %shard_map.81 = bf16[256,768]{1,0:T(8,128)(2,1)} custom-call(f32[256,768]{1,0:T(8,128)S(1)} %get-tuple-element.55.gated_ref, f32[4,2,128]{2,1,0:T(2,128)S(1)} %all-gather.1.square_ref, f32[1,768]{1,0:T(1,128)S(1)} %reshape.7.gain_ref), custom_call_target="tpu_custom_call" | custom-call | tf_op jit(solution)/shard_map/pallas_call | solution.py:306
  (16 shorter events, 0.1 us)
Async XLA Ops:
  1.1 3.8 %collective-permute-start = (bf16[256,1024]{1,0:T(8,128)(2,1)S(1)}, bf16[256,1024]{1,0:T(8,128)(2,1)S(1)}, u32[]{:S(2)}, u32[]{:S(2)}) collective-permute-start(bf16[256,1024]{1,0:T(8,128)(2,1)S(1)} %shard_map.73.own_ref), channel_id=1, source_target_pairs={{0,4},{4,0},{8,12},{12,8},{16,20},{20,16},{24,28},{28,24},{32,36},... | collective-permute-start | bytes 1572872 | tf_op jit(solution)/shard_map/ppermute | solution.py:326
  5.1 15.7 %collective-permute-start.1 = (bf16[512,256]{1,0:T(8,128)(2,1)S(1)}, bf16[512,256]{1,0:T(8,128)(2,1)S(1)}, u32[]{:S(2)}, u32[]{:S(2)}) collective-permute-start(bf16[512,256]{1,0:T(8,128)(2,1)S(1)} %get-tuple-element.32), channel_id=1, source_target_pairs={{0,24},{8,32},{16,40},{24,48},{32,56},{40,64},{48,72},{56,80},{64,... | collective-permute-start | bytes 786440 | tf_op jit(solution)/shard_map/ppermute | solution.py:322
  12.9 19.2 %collective-permute-start.5 = (bf16[512,256]{1,0:T(8,128)(2,1)S(1)}, bf16[512,256]{1,0:T(8,128)(2,1)S(1)}, u32[]{:S(2)}, u32[]{:S(2)}) collective-permute-start(bf16[512,256]{1,0:T(8,128)(2,1)S(1)} %get-tuple-element.32), channel_id=1, source_target_pairs={{0,8},{8,16},{16,24},{24,32},{32,40},{40,48},{48,56},{56,64},{64,7... | collective-permute-start | bytes 786440 | tf_op jit(solution)/shard_map/ppermute | solution.py:322
  20.9 17.5 %collective-permute-start.4 = (bf16[512,256]{1,0:T(8,128)(2,1)S(1)}, bf16[512,256]{1,0:T(8,128)(2,1)S(1)}, u32[]{:S(2)}, u32[]{:S(2)}) collective-permute-start(bf16[512,256]{1,0:T(8,128)(2,1)S(1)} %collective-permute-done.1.refs_3_), channel_id=1, source_target_pairs={{0,24},{8,32},{16,40},{24,48},{32,56},{40,64},{48,72},{56,80},{64,... | collective-permute-start | bytes 786440 | tf_op jit(solution)/shard_map/ppermute | solution.py:322
  26.8 15.7 %collective-permute-start.2 = (bf16[512,256]{1,0:T(8,128)(2,1)S(1)}, bf16[512,256]{1,0:T(8,128)(2,1)S(1)}, u32[]{:S(2)}, u32[]{:S(2)}) collective-permute-start(bf16[512,256]{1,0:T(8,128)(2,1)S(1)} %collective-permute-done.1.refs_3_), channel_id=1, source_target_pairs={{0,8},{8,16},{16,24},{24,32},{32,40},{40,48},{48,56},{56,64},{64,7... | collective-permute-start | bytes 786440 | tf_op jit(solution)/shard_map/ppermute | solution.py:322
  32.1 19.4 %collective-permute-start.8 = (bf16[512,256]{1,0:T(8,128)(2,1)S(1)}, bf16[512,256]{1,0:T(8,128)(2,1)S(1)}, u32[]{:S(2)}, u32[]{:S(2)}) collective-permute-start(bf16[512,256]{1,0:T(8,128)(2,1)S(1)} %collective-permute-done.5.refs_2_), channel_id=1, source_target_pairs={{0,8},{8,16},{16,24},{24,32},{32,40},{40,48},{48,56},{56,64},{64,7... | collective-permute-start | bytes 786440 | tf_op jit(solution)/shard_map/ppermute | solution.py:322
  38.4 20.9 %collective-permute-start.6 = (bf16[512,256]{1,0:T(8,128)(2,1)S(1)}, bf16[512,256]{1,0:T(8,128)(2,1)S(1)}, u32[]{:S(2)}, u32[]{:S(2)}) collective-permute-start(bf16[512,256]{1,0:T(8,128)(2,1)S(1)} %collective-permute-done.4.chunk_ref.refs_4_), channel_id=1, source_target_pairs={{0,8},{8,16},{16,24},{24,32},{32,40},{40,48},{48,56},{56,64},{64,7... | collective-permute-start | bytes 786440 | tf_op jit(solution)/shard_map/ppermute | solution.py:322
  42.5 16.7 %collective-permute-start.3 = (bf16[512,256]{1,0:T(8,128)(2,1)S(1)}, bf16[512,256]{1,0:T(8,128)(2,1)S(1)}, u32[]{:S(2)}, u32[]{:S(2)}) collective-permute-start(bf16[512,256]{1,0:T(8,128)(2,1)S(1)} %collective-permute-done.2.refs_3_), channel_id=1, source_target_pairs={{0,8},{8,16},{16,24},{24,32},{32,40},{40,48},{48,56},{56,64},{64,7... | collective-permute-start | bytes 786440 | tf_op jit(solution)/shard_map/ppermute | solution.py:322
  45.4 13.8 %collective-permute-start.7 = (bf16[256,256]{1,0:T(8,128)(2,1)S(1)}, bf16[256,256]{1,0:T(8,128)(2,1)S(1)}, u32[]{:S(2)}, u32[]{:S(2)}) collective-permute-start(bf16[256,256]{1,0:T(8,128)(2,1)S(1)} %shard_map.77), channel_id=1, source_target_pairs={{0,16},{8,24},{16,32},{24,40},{32,48},{40,56},{48,64},{56,72},{64,... | collective-permute-start | bytes 393224 | tf_op jit(solution)/shard_map/ppermute | solution.py:322
  59.3 8.3 %copy-start.2 = (f32[768]{0:T(1024)S(1)}, f32[768]{0:T(1024)}, u32[]{:S(2)}) copy-start(f32[768]{0:T(1024)} %param.13) | copy-start | bytes 9220
  59.3 10.0 %copy-start = (f32[4,768]{1,0:T(4,128)S(1)}, f32[4,768]{1,0:T(4,128)}, u32[]{:S(2)}) copy-start(f32[4,768]{1,0:T(4,128)} %gate_ref.1) | copy-start | bytes 36868
  59.3 10.0 %copy-start.1 = (s32[64]{0:T(128)S(1)}, s32[64]{0:T(128)}, u32[]{:S(2)}) copy-start(s32[64]{0:T(128)} %ids_ref.1) | copy-start | bytes 772
  65.6 3.7 %collective-permute-start.9 = (bf16[272,768]{1,0:T(8,128)(2,1)S(1)}, bf16[272,768]{1,0:T(8,128)(2,1)S(1)}, u32[]{:S(2)}, u32[]{:S(2)}) collective-permute-start(bf16[272,768]{1,0:T(8,128)(2,1)S(1)} %get-tuple-element.54), channel_id=1, source_target_pairs={{0,4},{4,0},{8,12},{12,8},{16,20},{20,16},{24,28},{28,24},{32,36},... | collective-permute-start | bytes 1253384 | tf_op jit(solution)/shard_map/ppermute | solution.py:326

commit v4 on v3

--- a/solution.py
+++ b/solution.py
@@ -173,7 +173,7 @@
     for slot in range(2):
         rows = slice(slot * BLOCK, (slot + 1) * BLOCK)
         gate_row = gate_ref[pl.ds(ids_ref[places[slot]], 1), :]
-        parts = theirs[2 * BLOCK + 8 * slot : 2 * BLOCK + 8 * slot + 8, :].astype(jnp.float32)
+        parts = theirs[2 * BLOCK :, :].astype(jnp.float32)[8 * slot : 8 * slot + 3]
         levels = parts[0:1] + parts[1:2] + parts[2:3]
         total = jnp.zeros((BLOCK, HEAD_DIM), jnp.float32)
         for head in range(LOCAL_HEADS):
@@ -342,21 +342,25 @@
         + [jnp.full((1, BLOCKS), frame, jnp.int32)],
         axis=0,
     )
-    s3 = send(chunk, 3)
+    s2 = send(chunk, 2)
     s1 = send(chunk, 1)
     state = attend([("own", 0)], [mine], meta, both, None)
-    s3, state = after(s3, state)
-    s6 = send(s3, 3)
-    s4 = send(s3, 1)
-    s2 = send(s1, 1)
-    state = attend([("whole", 1), ("whole", 3)], [s1, s3], meta, both, state)
+    s2, state = after(s2, state)
+    s4 = send(s2, 2)
+    s3 = send(s2, 1)
+    state = attend([("whole", 1), ("whole", 2)], [s1, s2], meta, both, state)
+    s4, state = after(s4, state)
+    s6 = send(s4, 2)
+    s5 = send(s4, 1)
+    state = attend([("whole", 3), ("whole", 4)], [s3, s4], meta, both, state)
     s6, state = after(s6, state)
+    half = half_of(here, s6)
+    half, s6 = lax.optimization_barrier((half, s6))
+    s8 = send(half, 2)
     s7 = send(s6, 1)
-    s8 = send(half_of(here, s6), 2)
-    s5 = send(s4, 1)
-    state = attend([("whole", 2), ("whole", 4), ("whole", 6)], [s2, s4, s6], meta, both, state)
+    state = attend([("whole", 5), ("whole", 6)], [s5, s6], meta, both, state)
     *state, theirs = attend(
-        [("whole", 5), ("whole", 7), ("half", 8)], [s5, s7, s8], meta, both, state, last=True
+        [("whole", 7), ("half", 8)], [s7, s8], meta, both, state, last=True
     )
     gated, squares = finish(meta, section_ids, section_gate, state, swap(theirs))
     squares = lax.all_gather(squares, "head", axis=0)

time: 80.8 us -> 80.7 us (level)
  the two profiles are of different devices: /device:TPU:160 before, /device:TPU:24 now
where the time goes in v4:
time: 80.7 us; the launch traced here: 80.2 us
  starting transfers between devices  38.3 us (47%)
  Pallas kernels  22 us (27%)
  blocking collectives  9.73 us (12%)
  waiting for transfers between devices  9.22 us (11%)
  local copies, waits for them, and re-layouts  0.82 us (1%)
    ppermute x8, starting transfers between devices, send(): return lax.ppermute(array, 'frame', along(hops))  34.4 us
    pallas_call x5, Pallas kernels, attend(): pl.pallas_call(functools.partial(attend_body, pieces, first, last), out_s...  18.3 us
    all_gather x1, blocking collectives, body(): squares = lax.all_gather(squares, 'head', axis=0)  9.73 us
    ppermute x8, waiting for transfers between devices, send(): return lax.ppermute(array, 'frame', along(hops))  5.65 us
    ppermute x2, starting transfers between devices, swap(): return lax.ppermute(array, 'frame', [(d, d ^ 1) for d in range(2 * CHIPS)])  3.84 us
    ppermute x2, waiting for transfers between devices, swap(): return lax.ppermute(array, 'frame', [(d, d ^ 1) for d in range(2 * CHIPS)])  3.57 us
  transfers between devices with their start and end apart: 10, of which 4 were waited for; matrix products, arithmetic and copies ran while one was open for 1% of the time, Pallas kernels for 19%

profile of v4, /device:TPU:24, one launch (start us, length us, event | category | flops | bytes accessed | tf_op | source)
XLA Modules:
  0.0 80.2 jit_solution(15647042368603626207)
XLA Ops:
  0.0 1.1 %shard_map.73.own_ref = bf16[256,1024]{1,0:T(8,128)(2,1)S(1)} custom-call(bf16[256,128]{1,0:T(8,128)(2,1)} %keys_ref.1, bf16[256,128]{1,0:T(8,128)(2,1)} %values_ref.1, bf16[256,768]{1,0:T(8,128)(2,1)} %queries_ref.1), custom_call_target="tpu_custom_call" | custom-call | tf_op jit(solution)/shard_map/pallas_call | solution.py:224
  1.1 1.9 %collective-permute-start = (bf16[256,1024]{1,0:T(8,128)(2,1)S(1)}, bf16[256,1024]{1,0:T(8,128)(2,1)S(1)}, u32[]{:S(2)}, u32[]{:S(2)}) collective-permute-start(bf16[256,1024]{1,0:T(8,128)(2,1)S(1)} %shard_map.73.own_ref), channel_id=1, source_target_pairs={{0,4},{4,0},{8,12},{12,8},{16,20},{20,16},{24,28},{28,24},{32,36},... | collective-permute-start | bytes 1572872 | tf_op jit(solution)/shard_map/ppermute | solution.py:326
  3.0 1.9 %collective-permute-done.other_ref = bf16[256,1024]{1,0:T(8,128)(2,1)S(1)} collective-permute-done((bf16[256,1024]{1,0:T(8,128)(2,1)S(1)}, bf16[256,1024]{1,0:T(8,128)(2,1)S(1)}, u32[]{:S(2)}, u32[]{:S(2)}) %collective-permute-start) | collective-permute-done | bytes 524320 | tf_op jit(solution)/shard_map/ppermute | solution.py:326
  5.1 5.2 %collective-permute-start.1 = (bf16[512,256]{1,0:T(8,128)(2,1)S(1)}, bf16[512,256]{1,0:T(8,128)(2,1)S(1)}, u32[]{:S(2)}, u32[]{:S(2)}) collective-permute-start(bf16[512,256]{1,0:T(8,128)(2,1)S(1)} %get-tuple-element.41), channel_id=1, source_target_pairs={{0,16},{8,24},{16,32},{24,40},{32,48},{40,56},{48,64},{56,72},{64,... | collective-permute-start | bytes 786440 | tf_op jit(solution)/shard_map/ppermute | solution.py:322
  10.3 3.8 %collective-permute-start.3 = (bf16[512,256]{1,0:T(8,128)(2,1)S(1)}, bf16[512,256]{1,0:T(8,128)(2,1)S(1)}, u32[]{:S(2)}, u32[]{:S(2)}) collective-permute-start(bf16[512,256]{1,0:T(8,128)(2,1)S(1)} %get-tuple-element.41), channel_id=1, source_target_pairs={{0,8},{8,16},{16,24},{24,32},{32,40},{40,48},{48,56},{56,64},{64,7... | collective-permute-start | bytes 786440 | tf_op jit(solution)/shard_map/ppermute | solution.py:322
  14.2 0.8 constant_dynamic-slice_fusion
  15.0 2.7 %shard_map.75 = (f32[512,768]{1,0:T(8,128)S(1)}, f32[512,768]{1,0:T(8,128)S(1)}, f32[512,768]{1,0:T(8,128)S(1)}) custom-call(s32[5,64]{1,0:T(8,128)S(1)} %concatenate.3.refs_0_.frame_ref, bf16[512,768]{1,0:T(8,128)(2,1)S(1)} %get-tuple-element.40.refs_1_, bf16[256,256]{1,0:T(8,128)(2,1)S(1)} %get-tuple-element.42.refs_2_), custom_call_target="tpu_custom_call" | custom-call | flops 402653184 | bytes 12582912 | tf_op jit(solution)/shard_map/pallas_call | solution.py:153
  17.7 4.2 %collective-permute-done.1.refs_3_ = bf16[512,256]{1,0:T(8,128)(2,1)S(1)} collective-permute-done((bf16[512,256]{1,0:T(8,128)(2,1)S(1)}, bf16[512,256]{1,0:T(8,128)(2,1)S(1)}, u32[]{:S(2)}, u32[]{:S(2)}) %collective-permute-start.1) | collective-permute-done | bytes 262176 | tf_op jit(solution)/shard_map/ppermute | solution.py:322
  21.9 2.2 %collective-permute-start.2 = (bf16[512,256]{1,0:T(8,128)(2,1)S(1)}, bf16[512,256]{1,0:T(8,128)(2,1)S(1)}, u32[]{:S(2)}, u32[]{:S(2)}) collective-permute-start(bf16[512,256]{1,0:T(8,128)(2,1)S(1)} %collective-permute-done.1.refs_3_), channel_id=1, source_target_pairs={{0,16},{8,24},{16,32},{24,40},{32,48},{40,56},{48,64},{56,72},{64,... | collective-permute-start | bytes 786440 | tf_op jit(solution)/shard_map/ppermute | solution.py:322
  24.1 4.8 %collective-permute-start.5 = (bf16[512,256]{1,0:T(8,128)(2,1)S(1)}, bf16[512,256]{1,0:T(8,128)(2,1)S(1)}, u32[]{:S(2)}, u32[]{:S(2)}) collective-permute-start(bf16[512,256]{1,0:T(8,128)(2,1)S(1)} %collective-permute-done.1.refs_3_), channel_id=1, source_target_pairs={{0,8},{8,16},{16,24},{24,32},{32,40},{40,48},{48,56},{56,64},{64,7... | collective-permute-start | bytes 786440 | tf_op jit(solution)/shard_map/ppermute | solution.py:322
  29.0 4.1 %shard_map.76 = (f32[512,768]{1,0:T(8,128)S(1)}, f32[512,768]{1,0:T(8,128)S(1)}, f32[512,768]{1,0:T(8,128)S(1)}) custom-call(s32[5,64]{1,0:T(8,128)S(1)} %concatenate.3.refs_0_.frame_ref, bf16[512,768]{1,0:T(8,128)(2,1)S(1)} %get-tuple-element.40.refs_1_, ...), custom_call_target="tpu_custom_call", output_to_operand_aliasing={{0}: (4, {}), {1}: (5, {}), {2}: (6, {})} | custom-call | flops 1610612736 | bytes 12582912 | tf_op jit(solution)/shard_map/pallas_call | solution.py:153
  33.1 3.8 %collective-permute-start.4 = (bf16[512,256]{1,0:T(8,128)(2,1)S(1)}, bf16[512,256]{1,0:T(8,128)(2,1)S(1)}, u32[]{:S(2)}, u32[]{:S(2)}) collective-permute-start(bf16[512,256]{1,0:T(8,128)(2,1)S(1)} %collective-permute-done.2.refs_3_), channel_id=1, source_target_pairs={{0,16},{8,24},{16,32},{24,40},{32,48},{40,56},{48,64},{56,72},{64,... | collective-permute-start | bytes 786440 | tf_op jit(solution)/shard_map/ppermute | solution.py:322
  36.9 4.3 %collective-permute-start.8 = (bf16[512,256]{1,0:T(8,128)(2,1)S(1)}, bf16[512,256]{1,0:T(8,128)(2,1)S(1)}, u32[]{:S(2)}, u32[]{:S(2)}) collective-permute-start(bf16[512,256]{1,0:T(8,128)(2,1)S(1)} %collective-permute-done.2.refs_3_), channel_id=1, source_target_pairs={{0,8},{8,16},{16,24},{24,32},{32,40},{40,48},{48,56},{56,64},{64,7... | collective-permute-start | bytes 786440 | tf_op jit(solution)/shard_map/ppermute | solution.py:322
  41.3 4.1 %shard_map.77 = (f32[512,768]{1,0:T(8,128)S(1)}, f32[512,768]{1,0:T(8,128)S(1)}, f32[512,768]{1,0:T(8,128)S(1)}) custom-call(s32[5,64]{1,0:T(8,128)S(1)} %concatenate.3.refs_0_.frame_ref, bf16[512,768]{1,0:T(8,128)(2,1)S(1)} %get-tuple-element.40.refs_1_, ...), custom_call_target="tpu_custom_call", output_to_operand_aliasing={{0}: (4, {}), {1}: (5, {}), {2}: (6, {})} | custom-call | flops 1610612736 | bytes 12582912 | tf_op jit(solution)/shard_map/pallas_call | solution.py:153
  45.6 4.4 %collective-permute-start.6 = (bf16[512,256]{1,0:T(8,128)(2,1)S(1)}, bf16[512,256]{1,0:T(8,128)(2,1)S(1)}, u32[]{:S(2)}, u32[]{:S(2)}) collective-permute-start(bf16[512,256]{1,0:T(8,128)(2,1)S(1)} %collective-permute-done.4.chunk_ref.refs_3_), channel_id=1, source_target_pairs={{0,8},{8,16},{16,24},{24,32},{32,40},{40,48},{48,56},{56,64},{64,7... | collective-permute-start | bytes 786440 | tf_op jit(solution)/shard_map/ppermute | solution.py:322
  50.0 5.8 %collective-permute-start.7 = (bf16[256,256]{1,0:T(8,128)(2,1)S(1)}, bf16[256,256]{1,0:T(8,128)(2,1)S(1)}, u32[]{:S(2)}, u32[]{:S(2)}) collective-permute-start(bf16[256,256]{1,0:T(8,128)(2,1)S(1)} %shard_map.78), channel_id=1, source_target_pairs={{0,16},{8,24},{16,32},{24,40},{32,48},{40,56},{48,64},{56,72},{64,... | collective-permute-start | bytes 393224 | tf_op jit(solution)/shard_map/ppermute | solution.py:322
  55.9 4.2 %shard_map.79 = (f32[512,768]{1,0:T(8,128)S(1)}, f32[512,768]{1,0:T(8,128)S(1)}, f32[512,768]{1,0:T(8,128)S(1)}) custom-call(s32[5,64]{1,0:T(8,128)S(1)} %concatenate.3.refs_0_.frame_ref, bf16[512,768]{1,0:T(8,128)(2,1)S(1)} %get-tuple-element.40.refs_1_, ...), custom_call_target="tpu_custom_call", output_to_operand_aliasing={{0}: (4, {}), {1}: (5, {}), {2}: (6, {})} | custom-call | flops 1610612736 | bytes 12582912 | tf_op jit(solution)/shard_map/pallas_call | solution.py:153
  60.1 1.4 %collective-permute-done.7.refs_3_ = bf16[256,256]{1,0:T(8,128)(2,1)S(1)} collective-permute-done((bf16[256,256]{1,0:T(8,128)(2,1)S(1)}, bf16[256,256]{1,0:T(8,128)(2,1)S(1)}, u32[]{:S(2)}, u32[]{:S(2)}) %collective-permute-start.7) | collective-permute-done | bytes 131104 | tf_op jit(solution)/shard_map/ppermute | solution.py:322
  61.5 3.1 %shard_map.80 = (f32[512,768]{1,0:T(8,128)S(1)}, f32[512,768]{1,0:T(8,128)S(1)}, f32[512,768]{1,0:T(8,128)S(1)}, bf16[272,768]{1,0:T(8,128)(2,1)S(1)}) custom-call(s32[5,64]{1,0:T(8,128)S(1)} %concatenate.3.refs_0_.frame_ref, bf16[512,768]{1,0:T(8,128)(2,1)S(1)} %get-tuple-element.40.refs_1_, ...), custom_call_target="tpu_custom_call", output_to_operand_aliasing={{0}: (4, {}), {1}: (5, {}), {2}: (6, {})} | custom-call | flops 1207959552 | bytes 12582912 | tf_op jit(solution)/shard_map/pallas_call | solution.py:153
  64.6 1.9 %collective-permute-start.9 = (bf16[272,768]{1,0:T(8,128)(2,1)S(1)}, bf16[272,768]{1,0:T(8,128)(2,1)S(1)}, u32[]{:S(2)}, u32[]{:S(2)}) collective-permute-start(bf16[272,768]{1,0:T(8,128)(2,1)S(1)} %get-tuple-element.72), channel_id=1, source_target_pairs={{0,4},{4,0},{8,12},{12,8},{16,20},{20,16},{24,28},{28,24},{32,36},... | collective-permute-start | bytes 1253384 | tf_op jit(solution)/shard_map/ppermute | solution.py:326
  66.6 1.7 %collective-permute-done.9.theirs = bf16[272,768]{1,0:T(8,128)(2,1)S(1)} collective-permute-done((bf16[272,768]{1,0:T(8,128)(2,1)S(1)}, bf16[272,768]{1,0:T(8,128)(2,1)S(1)}, u32[]{:S(2)}, u32[]{:S(2)}) %collective-permute-start.9) | collective-permute-done | bytes 417824 | tf_op jit(solution)/shard_map/ppermute | solution.py:326
  68.3 1.3 %shard_map.81 = (f32[256,768]{1,0:T(8,128)S(1)}, f32[2,128]{1,0:T(2,128)S(1)}) custom-call(s32[5,64]{1,0:T(8,128)S(1)} %concatenate.3.refs_0_.frame_ref, s32[64]{0:T(128)S(1)} %copy-done.1, f32[4,768]{1,0:T(4,128)S(1)} %copy-done, f32[512,768]{1,0:T(8,128)S(1)} %get-tuple-element.69.acc_ref, f32[512,768]{1,0:T(8,128)S(1)} %get-tuple-element.70.sum_ref, ...), custom_call_target="tpu_custom_call" | custom-call | tf_op jit(solution)/shard_map/pallas_call | solution.py:196
  69.6 9.7 %all-gather.1.square_ref = f32[4,2,128]{2,1,0:T(2,128)S(1)} all-gather(f32[1,2,128]{2,1,0:T(2,128)S(1)} %bitcast.2), channel_id=2, replica_groups=mesh['stream'=4,'frame'=32,'head'=4] {'head'}, dimensions={0}, use_global_device_ids=true | all-gather | bytes 5120 | tf_op jit(solution)/shard_map/all_gather | solution.py:366
  79.3 0.9 %shard_map.82 = bf16[256,768]{1,0:T(8,128)(2,1)} custom-call(f32[256,768]{1,0:T(8,128)S(1)} %get-tuple-element.73.gated_ref, f32[4,2,128]{2,1,0:T(2,128)S(1)} %all-gather.1.square_ref, f32[1,768]{1,0:T(1,128)S(1)} %reshape.7.gain_ref), custom_call_target="tpu_custom_call" | custom-call | tf_op jit(solution)/shard_map/pallas_call | solution.py:306
  (17 shorter events, 0.4 us)
Async XLA Ops:
  1.1 3.8 %collective-permute-start = (bf16[256,1024]{1,0:T(8,128)(2,1)S(1)}, bf16[256,1024]{1,0:T(8,128)(2,1)S(1)}, u32[]{:S(2)}, u32[]{:S(2)}) collective-permute-start(bf16[256,1024]{1,0:T(8,128)(2,1)S(1)} %shard_map.73.own_ref), channel_id=1, source_target_pairs={{0,4},{4,0},{8,12},{12,8},{16,20},{20,16},{24,28},{28,24},{32,36},... | collective-permute-start | bytes 1572872 | tf_op jit(solution)/shard_map/ppermute | solution.py:326
  5.1 16.8 %collective-permute-start.1 = (bf16[512,256]{1,0:T(8,128)(2,1)S(1)}, bf16[512,256]{1,0:T(8,128)(2,1)S(1)}, u32[]{:S(2)}, u32[]{:S(2)}) collective-permute-start(bf16[512,256]{1,0:T(8,128)(2,1)S(1)} %get-tuple-element.41), channel_id=1, source_target_pairs={{0,16},{8,24},{16,32},{24,40},{32,48},{40,56},{48,64},{56,72},{64,... | collective-permute-start | bytes 786440 | tf_op jit(solution)/shard_map/ppermute | solution.py:322
  10.3 18.7 %collective-permute-start.3 = (bf16[512,256]{1,0:T(8,128)(2,1)S(1)}, bf16[512,256]{1,0:T(8,128)(2,1)S(1)}, u32[]{:S(2)}, u32[]{:S(2)}) collective-permute-start(bf16[512,256]{1,0:T(8,128)(2,1)S(1)} %get-tuple-element.41), channel_id=1, source_target_pairs={{0,8},{8,16},{16,24},{24,32},{32,40},{40,48},{48,56},{56,64},{64,7... | collective-permute-start | bytes 786440 | tf_op jit(solution)/shard_map/ppermute | solution.py:322
  21.9 11.2 %collective-permute-start.2 = (bf16[512,256]{1,0:T(8,128)(2,1)S(1)}, bf16[512,256]{1,0:T(8,128)(2,1)S(1)}, u32[]{:S(2)}, u32[]{:S(2)}) collective-permute-start(bf16[512,256]{1,0:T(8,128)(2,1)S(1)} %collective-permute-done.1.refs_3_), channel_id=1, source_target_pairs={{0,16},{8,24},{16,32},{24,40},{32,48},{40,56},{48,64},{56,72},{64,... | collective-permute-start | bytes 786440 | tf_op jit(solution)/shard_map/ppermute | solution.py:322
  24.1 17.1 %collective-permute-start.5 = (bf16[512,256]{1,0:T(8,128)(2,1)S(1)}, bf16[512,256]{1,0:T(8,128)(2,1)S(1)}, u32[]{:S(2)}, u32[]{:S(2)}) collective-permute-start(bf16[512,256]{1,0:T(8,128)(2,1)S(1)} %collective-permute-done.1.refs_3_), channel_id=1, source_target_pairs={{0,8},{8,16},{16,24},{24,32},{32,40},{40,48},{48,56},{56,64},{64,7... | collective-permute-start | bytes 786440 | tf_op jit(solution)/shard_map/ppermute | solution.py:322
  33.1 12.3 %collective-permute-start.4 = (bf16[512,256]{1,0:T(8,128)(2,1)S(1)}, bf16[512,256]{1,0:T(8,128)(2,1)S(1)}, u32[]{:S(2)}, u32[]{:S(2)}) collective-permute-start(bf16[512,256]{1,0:T(8,128)(2,1)S(1)} %collective-permute-done.2.refs_3_), channel_id=1, source_target_pairs={{0,16},{8,24},{16,32},{24,40},{32,48},{40,56},{48,64},{56,72},{64,... | collective-permute-start | bytes 786440 | tf_op jit(solution)/shard_map/ppermute | solution.py:322
  36.9 18.9 %collective-permute-start.8 = (bf16[512,256]{1,0:T(8,128)(2,1)S(1)}, bf16[512,256]{1,0:T(8,128)(2,1)S(1)}, u32[]{:S(2)}, u32[]{:S(2)}) collective-permute-start(bf16[512,256]{1,0:T(8,128)(2,1)S(1)} %collective-permute-done.2.refs_3_), channel_id=1, source_target_pairs={{0,8},{8,16},{16,24},{24,32},{32,40},{40,48},{48,56},{56,64},{64,7... | collective-permute-start | bytes 786440 | tf_op jit(solution)/shard_map/ppermute | solution.py:322
  45.6 15.9 %collective-permute-start.6 = (bf16[512,256]{1,0:T(8,128)(2,1)S(1)}, bf16[512,256]{1,0:T(8,128)(2,1)S(1)}, u32[]{:S(2)}, u32[]{:S(2)}) collective-permute-start(bf16[512,256]{1,0:T(8,128)(2,1)S(1)} %collective-permute-done.4.chunk_ref.refs_3_), channel_id=1, source_target_pairs={{0,8},{8,16},{16,24},{24,32},{32,40},{40,48},{48,56},{56,64},{64,7... | collective-permute-start | bytes 786440 | tf_op jit(solution)/shard_map/ppermute | solution.py:322
  50.0 11.5 %collective-permute-start.7 = (bf16[256,256]{1,0:T(8,128)(2,1)S(1)}, bf16[256,256]{1,0:T(8,128)(2,1)S(1)}, u32[]{:S(2)}, u32[]{:S(2)}) collective-permute-start(bf16[256,256]{1,0:T(8,128)(2,1)S(1)} %shard_map.78), channel_id=1, source_target_pairs={{0,16},{8,24},{16,32},{24,40},{32,48},{40,56},{48,64},{56,72},{64,... | collective-permute-start | bytes 393224 | tf_op jit(solution)/shard_map/ppermute | solution.py:322
  61.5 5.1 %copy-start.2 = (f32[768]{0:T(1024)S(1)}, f32[768]{0:T(1024)}, u32[]{:S(2)}) copy-start(f32[768]{0:T(1024)} %param.13) | copy-start | bytes 9220
  61.5 6.8 %copy-start = (f32[4,768]{1,0:T(4,128)S(1)}, f32[4,768]{1,0:T(4,128)}, u32[]{:S(2)}) copy-start(f32[4,768]{1,0:T(4,128)} %gate_ref.1) | copy-start | bytes 36868
  61.5 6.8 %copy-start.1 = (s32[64]{0:T(128)S(1)}, s32[64]{0:T(128)}, u32[]{:S(2)}) copy-start(s32[64]{0:T(128)} %ids_ref.1) | copy-start | bytes 772
  64.6 3.7 %collective-permute-start.9 = (bf16[272,768]{1,0:T(8,128)(2,1)S(1)}, bf16[272,768]{1,0:T(8,128)(2,1)S(1)}, u32[]{:S(2)}, u32[]{:S(2)}) collective-permute-start(bf16[272,768]{1,0:T(8,128)(2,1)S(1)} %get-tuple-element.72), channel_id=1, source_target_pairs={{0,4},{4,0},{8,12},{12,8},{16,20},{20,16},{24,28},{28,24},{32,36},... | collective-permute-start | bytes 1253384 | tf_op jit(solution)/shard_map/ppermute | solution.py:326

commit v5 on v4

--- a/solution.py
+++ b/solution.py
@@ -20,7 +20,7 @@
 VMEM_BYTES = 16 * 1024 * 1024
 
 
-def attend_body(pieces, first, last, *refs):
+def attend_body(pieces, slots, first, last, *refs):
     refs = list(refs)
     meta, q_ref = refs.pop(0), refs.pop(0)
     arrays = [refs.pop(0) for _ in pieces]
@@ -103,7 +103,7 @@
 
             return carry
 
-        lax.fori_loop(0, 4, per_slot, 0)
+        lax.fori_loop(slots[0], slots[1], per_slot, 0)
 
     if last:
         eye = diagonal()
@@ -132,7 +132,7 @@
     )
 
 
-def attend(pieces, arrays, meta, queries, state, last=False):
+def attend(pieces, arrays, meta, queries, state, last=False, slots=(0, 4)):
     first = state is None
     tiles = sum(array.shape[0] // 256 for array in arrays)
     rows, cols = queries.shape
@@ -149,9 +149,9 @@
     if last:
         out_shape.append(jax.ShapeDtypeStruct((rows // 2 + 16, cols), jnp.bfloat16))
         scratch.append(pltpu.VMEM((16, cols), jnp.float32))
-    pairs = tiles * 4 * LOCAL_HEADS
-    return pl.pallas_call(
-        functools.partial(attend_body, pieces, first, last),
+    pairs = tiles * (slots[1] - slots[0]) * LOCAL_HEADS
+    return pl.pallas_call(
+        functools.partial(attend_body, pieces, slots, first, last),
         out_shape=out_shape,
         in_specs=in_specs,
         out_specs=[vmem] * len(out_shape),
@@ -359,10 +359,11 @@
     s8 = send(half, 2)
     s7 = send(s6, 1)
     state = attend([("whole", 5), ("whole", 6)], [s5, s6], meta, both, state)
-    *state, theirs = attend(
-        [("whole", 7), ("half", 8)], [s7, s8], meta, both, state, last=True
-    )
-    gated, squares = finish(meta, section_ids, section_gate, state, swap(theirs))
+    final = [("whole", 7), ("half", 8)]
+    *state, theirs = attend(final, [s7, s8], meta, both, state, last=True, slots=(2, 4))
+    theirs = swap(theirs)
+    state = attend(final, [s7, s8], meta, both, state, slots=(0, 2))
+    gated, squares = finish(meta, section_ids, section_gate, state, theirs)
     squares = lax.all_gather(squares, "head", axis=0)
     return scale_rows(gated, squares, norm_gain.reshape(1, -1))
 

time: 80.7 us -> 80 us (level)
  Pallas kernels: 22 us -> 17 us
  waiting for transfers between devices: 9.22 us -> 14 us
    ppermute x8, waiting for transfers between devices: 5.65 us -> 11.8 us  [send(): return lax.ppermute(array, 'frame', along(hops))]
    pallas_call x5 -> x6, Pallas kernels: 18.3 us -> 13.3 us  [attend(): pl.pallas_call(functools.partial(attend_body, pieces, slots, first, last)...]
    ppermute x2, waiting for transfers between devices: 3.57 us -> 2.25 us  [swap(): return lax.ppermute(array, 'frame', [(d, d ^ 1) for d in range(2 * CHIPS)])]
  transfers between devices with their start and end apart: 10 -> 10, of which waited for: 4 -> 6; matrix products, arithmetic and copies ran while one was open for 1% -> 1% of each run, Pallas kernels for 19% -> 14%
where the time goes in v5:
time: 80 us; the launch traced here: 79.6 us
  starting transfers between devices  37.8 us (47%)
  Pallas kernels  17 us (21%)
  waiting for transfers between devices  14 us (18%)
  blocking collectives  9.73 us (12%)
  local copies, waits for them, and re-layouts  0.83 us (1%)
    ppermute x8, starting transfers between devices, send(): return lax.ppermute(array, 'frame', along(hops))  33.9 us
    pallas_call x6, Pallas kernels, attend(): pl.pallas_call(functools.partial(attend_body, pieces, slots, first, last)...  13.3 us
    ppermute x8, waiting for transfers between devices, send(): return lax.ppermute(array, 'frame', along(hops))  11.8 us
    all_gather x1, blocking collectives, body(): squares = lax.all_gather(squares, 'head', axis=0)  9.73 us
    ppermute x2, starting transfers between devices, swap(): return lax.ppermute(array, 'frame', [(d, d ^ 1) for d in range(2 * CHIPS)])  3.84 us
    ppermute x2, waiting for transfers between devices, swap(): return lax.ppermute(array, 'frame', [(d, d ^ 1) for d in range(2 * CHIPS)])  2.25 us
  transfers between devices with their start and end apart: 10, of which 6 were waited for; matrix products, arithmetic and copies ran while one was open for 1% of the time, Pallas kernels for 14%

profile of v5, /device:TPU:24, one launch (start us, length us, event | category | flops | bytes accessed | tf_op | source)
XLA Modules:
  0.0 79.6 jit_solution(16225555393493829335)
XLA Ops:
  0.0 1.1 %shard_map.73.own_ref = bf16[256,1024]{1,0:T(8,128)(2,1)S(1)} custom-call(bf16[256,128]{1,0:T(8,128)(2,1)} %keys_ref.1, bf16[256,128]{1,0:T(8,128)(2,1)} %values_ref.1, bf16[256,768]{1,0:T(8,128)(2,1)} %queries_ref.1), custom_call_target="tpu_custom_call" | custom-call | tf_op jit(solution)/shard_map/pallas_call | solution.py:224
  1.1 1.9 %collective-permute-start = (bf16[256,1024]{1,0:T(8,128)(2,1)S(1)}, bf16[256,1024]{1,0:T(8,128)(2,1)S(1)}, u32[]{:S(2)}, u32[]{:S(2)}) collective-permute-start(bf16[256,1024]{1,0:T(8,128)(2,1)S(1)} %shard_map.73.own_ref), channel_id=1, source_target_pairs={{0,4},{4,0},{8,12},{12,8},{16,20},{20,16},{24,28},{28,24},{32,36},... | collective-permute-start | bytes 1572872 | tf_op jit(solution)/shard_map/ppermute | solution.py:326
  3.0 1.9 %collective-permute-done.other_ref = bf16[256,1024]{1,0:T(8,128)(2,1)S(1)} collective-permute-done((bf16[256,1024]{1,0:T(8,128)(2,1)S(1)}, bf16[256,1024]{1,0:T(8,128)(2,1)S(1)}, u32[]{:S(2)}, u32[]{:S(2)}) %collective-permute-start) | collective-permute-done | bytes 524320 | tf_op jit(solution)/shard_map/ppermute | solution.py:326
  5.1 5.2 %collective-permute-start.1 = (bf16[512,256]{1,0:T(8,128)(2,1)S(1)}, bf16[512,256]{1,0:T(8,128)(2,1)S(1)}, u32[]{:S(2)}, u32[]{:S(2)}) collective-permute-start(bf16[512,256]{1,0:T(8,128)(2,1)S(1)} %get-tuple-element.44), channel_id=1, source_target_pairs={{0,16},{8,24},{16,32},{24,40},{32,48},{40,56},{48,64},{56,72},{64,... | collective-permute-start | bytes 786440 | tf_op jit(solution)/shard_map/ppermute | solution.py:322
  10.3 3.8 %collective-permute-start.3 = (bf16[512,256]{1,0:T(8,128)(2,1)S(1)}, bf16[512,256]{1,0:T(8,128)(2,1)S(1)}, u32[]{:S(2)}, u32[]{:S(2)}) collective-permute-start(bf16[512,256]{1,0:T(8,128)(2,1)S(1)} %get-tuple-element.44), channel_id=1, source_target_pairs={{0,8},{8,16},{16,24},{24,32},{32,40},{40,48},{48,56},{56,64},{64,7... | collective-permute-start | bytes 786440 | tf_op jit(solution)/shard_map/ppermute | solution.py:322
  15.0 2.2 %shard_map.75 = (f32[512,768]{1,0:T(8,128)S(1)}, f32[512,768]{1,0:T(8,128)S(1)}, f32[512,768]{1,0:T(8,128)S(1)}) custom-call(s32[5,64]{1,0:T(8,128)S(1)} %concatenate.3.refs_0_.frame_ref, bf16[512,768]{1,0:T(8,128)(2,1)S(1)} %get-tuple-element.43.refs_1_, bf16[256,256]{1,0:T(8,128)(2,1)S(1)} %get-tuple-element.45.refs_2_), custom_call_target="tpu_custom_call" | custom-call | flops 402653184 | bytes 12582912 | tf_op jit(solution)/shard_map/pallas_call | solution.py:153
  17.1 4.8 %collective-permute-done.1.refs_3_ = bf16[512,256]{1,0:T(8,128)(2,1)S(1)} collective-permute-done((bf16[512,256]{1,0:T(8,128)(2,1)S(1)}, bf16[512,256]{1,0:T(8,128)(2,1)S(1)}, u32[]{:S(2)}, u32[]{:S(2)}) %collective-permute-start.1) | collective-permute-done | bytes 262176 | tf_op jit(solution)/shard_map/ppermute | solution.py:322
  21.9 2.2 %collective-permute-start.2 = (bf16[512,256]{1,0:T(8,128)(2,1)S(1)}, bf16[512,256]{1,0:T(8,128)(2,1)S(1)}, u32[]{:S(2)}, u32[]{:S(2)}) collective-permute-start(bf16[512,256]{1,0:T(8,128)(2,1)S(1)} %collective-permute-done.1.refs_3_), channel_id=1, source_target_pairs={{0,16},{8,24},{16,32},{24,40},{32,48},{40,56},{48,64},{56,72},{64,... | collective-permute-start | bytes 786440 | tf_op jit(solution)/shard_map/ppermute | solution.py:322
  24.1 4.8 %collective-permute-start.5 = (bf16[512,256]{1,0:T(8,128)(2,1)S(1)}, bf16[512,256]{1,0:T(8,128)(2,1)S(1)}, u32[]{:S(2)}, u32[]{:S(2)}) collective-permute-start(bf16[512,256]{1,0:T(8,128)(2,1)S(1)} %collective-permute-done.1.refs_3_), channel_id=1, source_target_pairs={{0,8},{8,16},{16,24},{24,32},{32,40},{40,48},{48,56},{56,64},{64,7... | collective-permute-start | bytes 786440 | tf_op jit(solution)/shard_map/ppermute | solution.py:322
  29.0 2.5 %shard_map.76 = (f32[512,768]{1,0:T(8,128)S(1)}, f32[512,768]{1,0:T(8,128)S(1)}, f32[512,768]{1,0:T(8,128)S(1)}) custom-call(s32[5,64]{1,0:T(8,128)S(1)} %concatenate.3.refs_0_.frame_ref, bf16[512,768]{1,0:T(8,128)(2,1)S(1)} %get-tuple-element.43.refs_1_, ...), custom_call_target="tpu_custom_call", output_to_operand_aliasing={{0}: (4, {}), {1}: (5, {}), {2}: (6, {})} | custom-call | flops 1610612736 | bytes 12582912 | tf_op jit(solution)/shard_map/pallas_call | solution.py:153
  31.4 0.9 %collective-permute-done.2.refs_3_ = bf16[512,256]{1,0:T(8,128)(2,1)S(1)} collective-permute-done((bf16[512,256]{1,0:T(8,128)(2,1)S(1)}, bf16[512,256]{1,0:T(8,128)(2,1)S(1)}, u32[]{:S(2)}, u32[]{:S(2)}) %collective-permute-start.2) | collective-permute-done | bytes 262176 | tf_op jit(solution)/shard_map/ppermute | solution.py:322
  32.4 5.1 %collective-permute-start.4 = (bf16[512,256]{1,0:T(8,128)(2,1)S(1)}, bf16[512,256]{1,0:T(8,128)(2,1)S(1)}, u32[]{:S(2)}, u32[]{:S(2)}) collective-permute-start(bf16[512,256]{1,0:T(8,128)(2,1)S(1)} %collective-permute-done.2.refs_3_), channel_id=1, source_target_pairs={{0,16},{8,24},{16,32},{24,40},{32,48},{40,56},{48,64},{56,72},{64,... | collective-permute-start | bytes 786440 | tf_op jit(solution)/shard_map/ppermute | solution.py:322
  37.5 3.0 %collective-permute-start.8 = (bf16[512,256]{1,0:T(8,128)(2,1)S(1)}, bf16[512,256]{1,0:T(8,128)(2,1)S(1)}, u32[]{:S(2)}, u32[]{:S(2)}) collective-permute-start(bf16[512,256]{1,0:T(8,128)(2,1)S(1)} %collective-permute-done.2.refs_3_), channel_id=1, source_target_pairs={{0,8},{8,16},{16,24},{24,32},{32,40},{40,48},{48,56},{56,64},{64,7... | collective-permute-start | bytes 786440 | tf_op jit(solution)/shard_map/ppermute | solution.py:322
  40.5 2.5 %shard_map.77 = (f32[512,768]{1,0:T(8,128)S(1)}, f32[512,768]{1,0:T(8,128)S(1)}, f32[512,768]{1,0:T(8,128)S(1)}) custom-call(s32[5,64]{1,0:T(8,128)S(1)} %concatenate.3.refs_0_.frame_ref, bf16[512,768]{1,0:T(8,128)(2,1)S(1)} %get-tuple-element.43.refs_1_, ...), custom_call_target="tpu_custom_call", output_to_operand_aliasing={{0}: (4, {}), {1}: (5, {}), {2}: (6, {})} | custom-call | flops 1610612736 | bytes 12582912 | tf_op jit(solution)/shard_map/pallas_call | solution.py:153
  43.8 6.2 %collective-permute-start.6 = (bf16[512,256]{1,0:T(8,128)(2,1)S(1)}, bf16[512,256]{1,0:T(8,128)(2,1)S(1)}, u32[]{:S(2)}, u32[]{:S(2)}) collective-permute-start(bf16[512,256]{1,0:T(8,128)(2,1)S(1)} %collective-permute-done.4.chunk_ref.refs_3_), channel_id=1, source_target_pairs={{0,8},{8,16},{16,24},{24,32},{32,40},{40,48},{48,56},{56,64},{64,7... | collective-permute-start | bytes 786440 | tf_op jit(solution)/shard_map/ppermute | solution.py:322
  50.0 3.6 %collective-permute-start.7 = (bf16[256,256]{1,0:T(8,128)(2,1)S(1)}, bf16[256,256]{1,0:T(8,128)(2,1)S(1)}, u32[]{:S(2)}, u32[]{:S(2)}) collective-permute-start(bf16[256,256]{1,0:T(8,128)(2,1)S(1)} %shard_map.78), channel_id=1, source_target_pairs={{0,16},{8,24},{16,32},{24,40},{32,48},{40,56},{48,64},{56,72},{64,... | collective-permute-start | bytes 393224 | tf_op jit(solution)/shard_map/ppermute | solution.py:322
  53.6 2.5 %shard_map.79 = (f32[512,768]{1,0:T(8,128)S(1)}, f32[512,768]{1,0:T(8,128)S(1)}, f32[512,768]{1,0:T(8,128)S(1)}) custom-call(s32[5,64]{1,0:T(8,128)S(1)} %concatenate.3.refs_0_.frame_ref, bf16[512,768]{1,0:T(8,128)(2,1)S(1)} %get-tuple-element.43.refs_1_, ...), custom_call_target="tpu_custom_call", output_to_operand_aliasing={{0}: (4, {}), {1}: (5, {}), {2}: (6, {})} | custom-call | flops 1610612736 | bytes 12582912 | tf_op jit(solution)/shard_map/pallas_call | solution.py:153
  56.1 5.4 %collective-permute-done.7.refs_3_ = bf16[256,256]{1,0:T(8,128)(2,1)S(1)} collective-permute-done((bf16[256,256]{1,0:T(8,128)(2,1)S(1)}, bf16[256,256]{1,0:T(8,128)(2,1)S(1)}, u32[]{:S(2)}, u32[]{:S(2)}) %collective-permute-start.7) | collective-permute-done | bytes 131104 | tf_op jit(solution)/shard_map/ppermute | solution.py:322
  61.5 2.4 %shard_map.80 = (f32[512,768]{1,0:T(8,128)S(1)}, f32[512,768]{1,0:T(8,128)S(1)}, f32[512,768]{1,0:T(8,128)S(1)}, bf16[272,768]{1,0:T(8,128)(2,1)S(1)}) custom-call(s32[5,64]{1,0:T(8,128)S(1)} %concatenate.3.refs_0_.frame_ref, bf16[512,768]{1,0:T(8,128)(2,1)S(1)} %get-tuple-element.43.refs_1_, ...), custom_call_target="tpu_custom_call", output_to_operand_aliasing={{0}: (4, {}), {1}: (5, {}), {2}: (6, {})} | custom-call | flops 603979776 | bytes 12582912 | tf_op jit(solution)/shard_map/pallas_call | solution.py:153
  63.9 1.9 %collective-permute-start.9 = (bf16[272,768]{1,0:T(8,128)(2,1)S(1)}, bf16[272,768]{1,0:T(8,128)(2,1)S(1)}, u32[]{:S(2)}, u32[]{:S(2)}) collective-permute-start(bf16[272,768]{1,0:T(8,128)(2,1)S(1)} %get-tuple-element.78), channel_id=1, source_target_pairs={{0,4},{4,0},{8,12},{12,8},{16,20},{20,16},{24,28},{28,24},{32,36},... | collective-permute-start | bytes 1253384 | tf_op jit(solution)/shard_map/ppermute | solution.py:326
  65.9 1.3 %shard_map.81 = (f32[512,768]{1,0:T(8,128)S(1)}, f32[512,768]{1,0:T(8,128)S(1)}, f32[512,768]{1,0:T(8,128)S(1)}) custom-call(s32[5,64]{1,0:T(8,128)S(1)} %concatenate.3.refs_0_.frame_ref, bf16[512,768]{1,0:T(8,128)(2,1)S(1)} %get-tuple-element.43.refs_1_, ...), custom_call_target="tpu_custom_call", output_to_operand_aliasing={{0}: (4, {}), {1}: (5, {}), {2}: (6, {})} | custom-call | flops 603979776 | bytes 12582912 | tf_op jit(solution)/shard_map/pallas_call | solution.py:153
  67.6 1.3 %shard_map.82 = (f32[256,768]{1,0:T(8,128)S(1)}, f32[2,128]{1,0:T(2,128)S(1)}) custom-call(s32[5,64]{1,0:T(8,128)S(1)} %concatenate.3.refs_0_.frame_ref, s32[64]{0:T(128)S(1)} %copy-done.1, f32[4,768]{1,0:T(4,128)S(1)} %copy-done, f32[512,768]{1,0:T(8,128)S(1)} %get-tuple-element.75.acc_ref, f32[512,768]{1,0:T(8,128)S(1)} %get-tuple-element.76.sum_ref, ...), custom_call_target="tpu_custom_call" | custom-call | tf_op jit(solution)/shard_map/pallas_call | solution.py:196
  68.9 9.7 %all-gather.1.square_ref = f32[4,2,128]{2,1,0:T(2,128)S(1)} all-gather(f32[1,2,128]{2,1,0:T(2,128)S(1)} %bitcast.2), channel_id=2, replica_groups=mesh['stream'=4,'frame'=32,'head'=4] {'head'}, dimensions={0}, use_global_device_ids=true | all-gather | bytes 5120 | tf_op jit(solution)/shard_map/all_gather | solution.py:367
  78.7 0.9 %shard_map.83 = bf16[256,768]{1,0:T(8,128)(2,1)} custom-call(f32[256,768]{1,0:T(8,128)S(1)} %get-tuple-element.79.gated_ref, f32[4,2,128]{2,1,0:T(2,128)S(1)} %all-gather.1.square_ref, f32[1,768]{1,0:T(1,128)S(1)} %reshape.7.gain_ref), custom_call_target="tpu_custom_call" | custom-call | tf_op jit(solution)/shard_map/pallas_call | solution.py:306
  (18 shorter events, 2.3 us)
Async XLA Ops:
  1.1 3.8 %collective-permute-start = (bf16[256,1024]{1,0:T(8,128)(2,1)S(1)}, bf16[256,1024]{1,0:T(8,128)(2,1)S(1)}, u32[]{:S(2)}, u32[]{:S(2)}) collective-permute-start(bf16[256,1024]{1,0:T(8,128)(2,1)S(1)} %shard_map.73.own_ref), channel_id=1, source_target_pairs={{0,4},{4,0},{8,12},{12,8},{16,20},{20,16},{24,28},{28,24},{32,36},... | collective-permute-start | bytes 1572872 | tf_op jit(solution)/shard_map/ppermute | solution.py:326
  5.1 16.8 %collective-permute-start.1 = (bf16[512,256]{1,0:T(8,128)(2,1)S(1)}, bf16[512,256]{1,0:T(8,128)(2,1)S(1)}, u32[]{:S(2)}, u32[]{:S(2)}) collective-permute-start(bf16[512,256]{1,0:T(8,128)(2,1)S(1)} %get-tuple-element.44), channel_id=1, source_target_pairs={{0,16},{8,24},{16,32},{24,40},{32,48},{40,56},{48,64},{56,72},{64,... | collective-permute-start | bytes 786440 | tf_op jit(solution)/shard_map/ppermute | solution.py:322
  10.3 18.7 %collective-permute-start.3 = (bf16[512,256]{1,0:T(8,128)(2,1)S(1)}, bf16[512,256]{1,0:T(8,128)(2,1)S(1)}, u32[]{:S(2)}, u32[]{:S(2)}) collective-permute-start(bf16[512,256]{1,0:T(8,128)(2,1)S(1)} %get-tuple-element.44), channel_id=1, source_target_pairs={{0,8},{8,16},{16,24},{24,32},{32,40},{40,48},{48,56},{56,64},{64,7... | collective-permute-start | bytes 786440 | tf_op jit(solution)/shard_map/ppermute | solution.py:322
  21.9 10.5 %collective-permute-start.2 = (bf16[512,256]{1,0:T(8,128)(2,1)S(1)}, bf16[512,256]{1,0:T(8,128)(2,1)S(1)}, u32[]{:S(2)}, u32[]{:S(2)}) collective-permute-start(bf16[512,256]{1,0:T(8,128)(2,1)S(1)} %collective-permute-done.1.refs_3_), channel_id=1, source_target_pairs={{0,16},{8,24},{16,32},{24,40},{32,48},{40,56},{48,64},{56,72},{64,... | collective-permute-start | bytes 786440 | tf_op jit(solution)/shard_map/ppermute | solution.py:322
  24.1 16.3 %collective-permute-start.5 = (bf16[512,256]{1,0:T(8,128)(2,1)S(1)}, bf16[512,256]{1,0:T(8,128)(2,1)S(1)}, u32[]{:S(2)}, u32[]{:S(2)}) collective-permute-start(bf16[512,256]{1,0:T(8,128)(2,1)S(1)} %collective-permute-done.1.refs_3_), channel_id=1, source_target_pairs={{0,8},{8,16},{16,24},{24,32},{32,40},{40,48},{48,56},{56,64},{64,7... | collective-permute-start | bytes 786440 | tf_op jit(solution)/shard_map/ppermute | solution.py:322
  32.4 11.3 %collective-permute-start.4 = (bf16[512,256]{1,0:T(8,128)(2,1)S(1)}, bf16[512,256]{1,0:T(8,128)(2,1)S(1)}, u32[]{:S(2)}, u32[]{:S(2)}) collective-permute-start(bf16[512,256]{1,0:T(8,128)(2,1)S(1)} %collective-permute-done.2.refs_3_), channel_id=1, source_target_pairs={{0,16},{8,24},{16,32},{24,40},{32,48},{40,56},{48,64},{56,72},{64,... | collective-permute-start | bytes 786440 | tf_op jit(solution)/shard_map/ppermute | solution.py:322
  37.5 16.1 %collective-permute-start.8 = (bf16[512,256]{1,0:T(8,128)(2,1)S(1)}, bf16[512,256]{1,0:T(8,128)(2,1)S(1)}, u32[]{:S(2)}, u32[]{:S(2)}) collective-permute-start(bf16[512,256]{1,0:T(8,128)(2,1)S(1)} %collective-permute-done.2.refs_3_), channel_id=1, source_target_pairs={{0,8},{8,16},{16,24},{24,32},{32,40},{40,48},{48,56},{56,64},{64,7... | collective-permute-start | bytes 786440 | tf_op jit(solution)/shard_map/ppermute | solution.py:322
  43.8 17.7 %collective-permute-start.6 = (bf16[512,256]{1,0:T(8,128)(2,1)S(1)}, bf16[512,256]{1,0:T(8,128)(2,1)S(1)}, u32[]{:S(2)}, u32[]{:S(2)}) collective-permute-start(bf16[512,256]{1,0:T(8,128)(2,1)S(1)} %collective-permute-done.4.chunk_ref.refs_3_), channel_id=1, source_target_pairs={{0,8},{8,16},{16,24},{24,32},{32,40},{40,48},{48,56},{56,64},{64,7... | collective-permute-start | bytes 786440 | tf_op jit(solution)/shard_map/ppermute | solution.py:322
  50.0 11.5 %collective-permute-start.7 = (bf16[256,256]{1,0:T(8,128)(2,1)S(1)}, bf16[256,256]{1,0:T(8,128)(2,1)S(1)}, u32[]{:S(2)}, u32[]{:S(2)}) collective-permute-start(bf16[256,256]{1,0:T(8,128)(2,1)S(1)} %shard_map.78), channel_id=1, source_target_pairs={{0,16},{8,24},{16,32},{24,40},{32,48},{40,56},{48,64},{56,72},{64,... | collective-permute-start | bytes 393224 | tf_op jit(solution)/shard_map/ppermute | solution.py:322
  61.5 4.4 %copy-start.2 = (f32[768]{0:T(1024)S(1)}, f32[768]{0:T(1024)}, u32[]{:S(2)}) copy-start(f32[768]{0:T(1024)} %param.13) | copy-start | bytes 9220
  63.9 3.7 %collective-permute-start.9 = (bf16[272,768]{1,0:T(8,128)(2,1)S(1)}, bf16[272,768]{1,0:T(8,128)(2,1)S(1)}, u32[]{:S(2)}, u32[]{:S(2)}) collective-permute-start(bf16[272,768]{1,0:T(8,128)(2,1)S(1)} %get-tuple-element.78), channel_id=1, source_target_pairs={{0,4},{4,0},{8,12},{12,8},{16,20},{20,16},{24,28},{28,24},{32,36},... | collective-permute-start | bytes 1253384 | tf_op jit(solution)/shard_map/ppermute | solution.py:326
  65.9 1.7 %copy-start = (f32[4,768]{1,0:T(4,128)S(1)}, f32[4,768]{1,0:T(4,128)}, u32[]{:S(2)}) copy-start(f32[4,768]{1,0:T(4,128)} %gate_ref.1) | copy-start | bytes 36868
  65.9 1.7 %copy-start.1 = (s32[64]{0:T(128)S(1)}, s32[64]{0:T(128)}, u32[]{:S(2)}) copy-start(s32[64]{0:T(128)} %ids_ref.1) | copy-start | bytes 772
